TPU v7x, 32 devices: a whole 2x2x4 slice. The times are simulated.
32 devices in a mesh: dp: 4 (over y, x), fsdp: 8 (over z, core).
Axes of the slice: x: 2, y: 2, z: 4, core: 2. Of those that a mesh axis runs over, the one named last changes fastest.
Arguments:
- tokens: bfloat16 [49152, 768], P(('dp', 'fsdp')), may hold values from -6 to 6
- doc_lengths: int32 [96, 16], P(('dp', 'fsdp')), may hold values from 0 to 512, as said below
- params: bfloat16 [4464640], P(('dp', 'fsdp')), as said below
- cotangent: bfloat16 [49152, 768], P(('dp', 'fsdp')), may hold values from -6 to 6
Outputs:
- output: bfloat16 [49152, 768], P(('dp', 'fsdp'))
- grad_tokens: bfloat16 [49152, 768], P(('dp', 'fsdp'))
- grad_params: float32 [4464640], P(('dp', 'fsdp'))
Inputs may be any that keep to these rules, and one draw needn't show every extreme that they name: Row r holds its documents in order from its first position, doc_lengths[r, j] tokens in slot j (0 for an unused slot); a row's lengths sum to at most 512 and the rest of the row is padding; some row holds one document of 512 tokens. params holds, flattened row-major and in this order: proj_four [4, 768, 384] (query, key, value and convolution-value projections), point_w [768, 384], dense_w [768, 768], ffn_in [2, 384, 1536], ffn_out [2, 1536, 384], depth_w [9, 768], kernel_w [384, 54], query_bias, value_bias, conv_bias, point_bias (each 384), kernel_bias (54), dense_bias, norm1_gain, norm1_shift (each 768), ffn_in_bias (3072), ffn_out_bias, norm2_gain, norm2_shift (each 768); entries after 4460598 are unused.
All inputs are finite; a program needn't handle non-finite values.
Results may differ from a plain program's by a relative error of at most 0.02.
Values may be sent and summed in bfloat16 or wider, within the bound.
A program may use at most 320 MiB of HBM per device.

v0:
```python
from functools import partial
import math

import jax
import jax.numpy as jnp
from jax import lax
from jax.sharding import PartitionSpec as P

D = 768
HEADS = 6
HEAD_DIM = 64
FF = 3072
GROUPS = 2
KS = 9


EPS = 1e-12


def layout_table():
    att_width = HEADS * HEAD_DIM
    return [
        ("proj_four", (4, D, att_width)),
        ("point_w", (D, att_width)),
        ("dense_w", (D, D)),
        ("ffn_in", (GROUPS, D // GROUPS, FF // GROUPS)),
        ("ffn_out", (GROUPS, FF // GROUPS, D // GROUPS)),
        ("depth_w", (KS, D)),
        ("kernel_w", (att_width, HEADS * KS)),
        ("query_bias", (att_width,)),
        ("value_bias", (att_width,)),
        ("conv_bias", (att_width,)),
        ("point_bias", (att_width,)),
        ("kernel_bias", (HEADS * KS,)),
        ("dense_bias", (D,)),
        ("norm1_gain", (D,)),
        ("norm1_shift", (D,)),
        ("ffn_in_bias", (FF,)),
        ("ffn_out_bias", (D,)),
        ("norm2_gain", (D,)),
        ("norm2_shift", (D,)),
    ]


def unpack(flat_values):
    result = {}
    offset = 0
    for piece_name, piece_shape in layout_table():
        piece_size = math.prod(piece_shape)
        result[piece_name] = flat_values[offset : offset + piece_size].reshape(piece_shape)
        offset += piece_size
    return result


def layer_norm(values, gain, shift):
    centre = jnp.mean(values, axis=-1, keepdims=True)
    centred = values - centre
    variance = jnp.mean(centred * centred, axis=-1, keepdims=True)
    return centred * lax.rsqrt(variance + EPS) * gain + shift


def tap_softmax(tap_logits):
    return jax.nn.softmax(tap_logits, axis=-1)


def shift_rows(values, offset):
    length = values.shape[1]
    padded = jnp.pad(values, ((0, 0), (KS, KS), (0, 0)))
    return lax.slice_in_dim(padded, KS + offset, KS + offset + length, axis=1)


def shift_ids(doc_ids, offset):
    length = doc_ids.shape[1]
    padded = jnp.pad(doc_ids, ((0, 0), (KS, KS)), constant_values=-1)
    return lax.slice_in_dim(padded, KS + offset, KS + offset + length, axis=1)


def doc_numbers(doc_lengths, length):
    ends = jnp.cumsum(doc_lengths, axis=1)
    positions = jnp.arange(length, dtype=jnp.int32)
    doc_ids = jnp.sum((positions[None, :, None] >= ends[:, None, :]).astype(jnp.int32), axis=-1)
    valid_mask = (positions[None, :] < ends[:, -1:]).astype(jnp.float32)
    return (doc_ids, valid_mask)


def shards(tokens, doc_lengths, params, cotangent):
    f32 = jnp.float32
    bf16 = jnp.bfloat16
    att_width = HEADS * HEAD_DIM
    half_taps = KS // 2
    score_scale = HEAD_DIM ** (-0.5)
    row_count = doc_lengths.shape[0]
    token_count = tokens.shape[0]
    length = token_count // row_count
    gathered = lax.all_gather(params, ("dp", "fsdp"), axis=0, tiled=True)
    weights = unpack(gathered)

    def vector(piece_name):
        return weights[piece_name].astype(f32)

    doc_ids, valid_mask = doc_numbers(doc_lengths, length)
    tap_masks = [
        (shift_ids(doc_ids, tap_index - half_taps) == doc_ids).astype(f32)[:, :, None]
        for tap_index in range(KS)
    ]
    hidden32 = tokens.astype(f32).reshape(row_count, length, D)
    projected = jnp.einsum("td,mda->tma", tokens, weights["proj_four"], preferred_element_type=f32)
    queries = (projected[:, 0] + vector("query_bias")).astype(bf16)
    keys_low = projected[:, 1].astype(bf16)
    values = (projected[:, 2] + vector("value_bias")).astype(bf16)
    conv_vals = (projected[:, 3] + vector("conv_bias")).astype(bf16)
    depth_w = vector("depth_w")
    depth_conv = sum(
        (
            depth_w[tap_index] * shift_rows(hidden32, tap_index - half_taps) * tap_masks[tap_index]
            for tap_index in range(KS)
        )
    )
    depth_low = depth_conv.astype(bf16).reshape(token_count, D)
    keyconv = jnp.dot(depth_low, weights["point_w"], preferred_element_type=f32) + vector(
        "point_bias"
    )
    queries32 = queries.astype(f32)
    conv_attn = (keyconv * queries32).astype(bf16)
    logits = jnp.dot(conv_attn, weights["kernel_w"], preferred_element_type=f32) + vector(
        "kernel_bias"
    )
    tap_weights, taps_back = jax.vjp(tap_softmax, logits.reshape(row_count, length, HEADS, KS))
    conv32 = conv_vals.astype(f32).reshape(row_count, length, att_width)
    conv_out = sum(
        (
            tap_weights[..., tap_index : tap_index + 1]
            * (shift_rows(conv32, tap_index - half_taps) * tap_masks[tap_index]).reshape(
                row_count, length, HEADS, HEAD_DIM
            )
            for tap_index in range(KS)
        )
    )
    query_heads = queries.reshape(row_count, length, HEADS, HEAD_DIM)
    key_heads = keys_low.reshape(row_count, length, HEADS, HEAD_DIM)
    value_heads = values.reshape(row_count, length, HEADS, HEAD_DIM)

    def row_scores(row_query, row_key, row_ids):
        allowed = row_ids[:, None] == row_ids[None, :]
        scores = (
            jnp.einsum("qhd,khd->hqk", row_query, row_key, preferred_element_type=f32) * score_scale
        )
        return jnp.where(allowed[None], scores, -1e30)

    def attend(row_parts):
        row_query, row_key, row_value, row_ids = row_parts
        scores = row_scores(row_query, row_key, row_ids)
        row_max = jnp.max(scores, axis=-1, keepdims=True)
        exp_scores = jnp.exp(scores - row_max)
        row_total = jnp.sum(exp_scores, axis=-1, keepdims=True)
        probs_low = (exp_scores / row_total).astype(bf16)
        row_context = jnp.einsum("hqk,khd->qhd", probs_low, row_value, preferred_element_type=f32)
        return (row_context, row_max + jnp.log(row_total))

    context, log_totals = lax.map(attend, (query_heads, key_heads, value_heads, doc_ids))
    joined = jnp.concatenate(
        [context.reshape(token_count, att_width), conv_out.reshape(token_count, att_width)], axis=-1
    ).astype(bf16)
    first_sum = (
        jnp.dot(joined, weights["dense_w"], preferred_element_type=f32)
        + vector("dense_bias")
        + tokens.astype(f32)
    )
    normed, norm1_back = jax.vjp(layer_norm, first_sum, vector("norm1_gain"), vector("norm1_shift"))
    normed_low = normed.astype(bf16).reshape(token_count, GROUPS, D // GROUPS)
    inner_sum = jnp.einsum(
        "tgi,gio->tgo", normed_low, weights["ffn_in"], preferred_element_type=f32
    ).reshape(token_count, FF) + vector("ffn_in_bias")
    active, gelu_back = jax.vjp(partial(jax.nn.gelu, approximate=False), inner_sum)
    active_low = active.astype(bf16).reshape(token_count, GROUPS, FF // GROUPS)
    second = (
        jnp.einsum(
            "tgi,gio->tgo", active_low, weights["ffn_out"], preferred_element_type=f32
        ).reshape(token_count, D)
        + vector("ffn_out_bias")
        + normed
    )
    final_norm, norm2_back = jax.vjp(
        layer_norm, second, vector("norm2_gain"), vector("norm2_shift")
    )
    valid_flat = valid_mask.reshape(token_count, 1)
    output = (final_norm * valid_flat).astype(bf16)
    weights_back = unpack(lax.all_gather(params, ("dp", "fsdp"), axis=0, tiled=True))
    grad_final = cotangent.astype(f32) * valid_flat
    grad_second, grad_norm2_gain, grad_norm2_shift = norm2_back(grad_final)
    grad_second_low = grad_second.astype(bf16).reshape(token_count, GROUPS, D // GROUPS)
    grad_ffn_out = jnp.einsum(
        "tgi,tgo->gio", active_low, grad_second_low, preferred_element_type=f32
    )
    grad_ffn_out_bias = jnp.sum(grad_second, axis=0)
    grad_active = jnp.einsum(
        "tgo,gio->tgi", grad_second_low, weights_back["ffn_out"], preferred_element_type=f32
    ).reshape(token_count, FF)
    (grad_inner,) = gelu_back(grad_active)
    grad_inner_low = grad_inner.astype(bf16).reshape(token_count, GROUPS, FF // GROUPS)
    grad_ffn_in = jnp.einsum("tgi,tgo->gio", normed_low, grad_inner_low, preferred_element_type=f32)
    grad_ffn_in_bias = jnp.sum(grad_inner, axis=0)
    grad_normed = grad_second + jnp.einsum(
        "tgo,gio->tgi", grad_inner_low, weights_back["ffn_in"], preferred_element_type=f32
    ).reshape(token_count, D)
    grad_first, grad_norm1_gain, grad_norm1_shift = norm1_back(grad_normed)
    grad_first_low = grad_first.astype(bf16)
    grad_dense_w = jnp.einsum("ti,to->io", joined, grad_first_low, preferred_element_type=f32)
    grad_dense_bias = jnp.sum(grad_first, axis=0)
    grad_joined = jnp.einsum(
        "to,io->ti", grad_first_low, weights_back["dense_w"], preferred_element_type=f32
    )
    grad_context = (
        grad_joined[:, :att_width].astype(bf16).reshape(row_count, length, HEADS, HEAD_DIM)
    )
    grad_conv_out = grad_joined[:, att_width:].reshape(row_count, length, HEADS, HEAD_DIM)
    grad_taps = jnp.stack(
        [
            jnp.sum(
                grad_conv_out
                * (shift_rows(conv32, tap_index - half_taps) * tap_masks[tap_index]).reshape(
                    row_count, length, HEADS, HEAD_DIM
                ),
                axis=-1,
            )
            for tap_index in range(KS)
        ],
        axis=-1,
    )
    grad_conv = sum(
        (
            shift_rows(
                (tap_weights[..., tap_index : tap_index + 1] * grad_conv_out).reshape(
                    row_count, length, att_width
                )
                * tap_masks[tap_index],
                half_taps - tap_index,
            )
            for tap_index in range(KS)
        )
    )
    grad_conv = grad_conv.reshape(token_count, att_width)
    (grad_logits,) = taps_back(grad_taps)
    grad_logits = grad_logits.reshape(token_count, HEADS * KS)
    grad_kernel_bias = jnp.sum(grad_logits, axis=0)
    grad_logits_low = grad_logits.astype(bf16)
    grad_kernel_w = jnp.einsum("ta,tk->ak", conv_attn, grad_logits_low, preferred_element_type=f32)
    grad_conv_attn = jnp.einsum(
        "tk,ak->ta", grad_logits_low, weights_back["kernel_w"], preferred_element_type=f32
    )
    grad_keyconv = grad_conv_attn * queries32
    grad_point_bias = jnp.sum(grad_keyconv, axis=0)
    grad_keyconv_low = grad_keyconv.astype(bf16)
    grad_point_w = jnp.einsum("td,ta->da", depth_low, grad_keyconv_low, preferred_element_type=f32)
    grad_depth = jnp.einsum(
        "ta,da->td", grad_keyconv_low, weights_back["point_w"], preferred_element_type=f32
    ).reshape(row_count, length, D)
    grad_depth_w = jnp.stack(
        [
            jnp.sum(
                grad_depth * shift_rows(hidden32, tap_index - half_taps) * tap_masks[tap_index],
                axis=(0, 1),
            )
            for tap_index in range(KS)
        ],
        axis=0,
    )
    depth_back = weights_back["depth_w"].astype(f32)
    grad_hidden_depth = sum(
        (
            shift_rows(
                depth_back[tap_index] * grad_depth * tap_masks[tap_index], half_taps - tap_index
            )
            for tap_index in range(KS)
        )
    )

    def attend_back(row_parts):
        row_query, row_key, row_value, row_ids, row_lse, row_grad = row_parts
        scores = row_scores(row_query, row_key, row_ids)
        probs = jnp.exp(scores - row_lse)
        grad_probs = jnp.einsum("qhd,khd->hqk", row_grad, row_value, preferred_element_type=f32)
        inner_dot = jnp.sum(probs * grad_probs, axis=-1, keepdims=True)
        grad_scores = (probs * (grad_probs - inner_dot)).astype(bf16)
        grad_q = (
            jnp.einsum("hqk,khd->qhd", grad_scores, row_key, preferred_element_type=f32)
            * score_scale
        )
        grad_k = (
            jnp.einsum("hqk,qhd->khd", grad_scores, row_query, preferred_element_type=f32)
            * score_scale
        )
        grad_v = jnp.einsum(
            "hqk,qhd->khd", probs.astype(bf16), row_grad, preferred_element_type=f32
        )
        return (grad_q, grad_k, grad_v)

    grad_query_att, grad_keys, grad_values = lax.map(
        attend_back, (query_heads, key_heads, value_heads, doc_ids, log_totals, grad_context)
    )
    grad_query = grad_query_att.reshape(token_count, att_width) + grad_conv_attn * keyconv
    grad_keys = grad_keys.reshape(token_count, att_width)
    grad_values = grad_values.reshape(token_count, att_width)
    grad_four_low = jnp.stack([grad_query, grad_keys, grad_values, grad_conv], axis=1).astype(bf16)
    grad_proj_four = jnp.einsum("td,tma->mda", tokens, grad_four_low, preferred_element_type=f32)
    grad_tokens = (
        grad_first
        + grad_hidden_depth.reshape(token_count, D)
        + jnp.einsum(
            "tma,mda->td", grad_four_low, weights_back["proj_four"], preferred_element_type=f32
        )
    )
    gradients = {
        "proj_four": grad_proj_four,
        "point_w": grad_point_w,
        "dense_w": grad_dense_w,
        "ffn_in": grad_ffn_in,
        "ffn_out": grad_ffn_out,
        "depth_w": grad_depth_w,
        "kernel_w": grad_kernel_w,
        "query_bias": jnp.sum(grad_query, axis=0),
        "value_bias": jnp.sum(grad_values, axis=0),
        "conv_bias": jnp.sum(grad_conv, axis=0),
        "point_bias": grad_point_bias,
        "kernel_bias": grad_kernel_bias,
        "dense_bias": grad_dense_bias,
        "norm1_gain": grad_norm1_gain,
        "norm1_shift": grad_norm1_shift,
        "ffn_in_bias": grad_ffn_in_bias,
        "ffn_out_bias": grad_ffn_out_bias,
        "norm2_gain": grad_norm2_gain,
        "norm2_shift": grad_norm2_shift,
    }
    pieces = [gradients[piece_name].reshape(-1) for piece_name, piece_shape in layout_table()]
    used_size = sum((math.prod(piece_shape) for piece_name, piece_shape in layout_table()))
    flat_grad = jnp.concatenate(pieces + [jnp.zeros((gathered.shape[0] - used_size,), f32)])
    outer_count = lax.axis_size("dp")
    inner_count = lax.axis_size("fsdp")
    shard_len = flat_grad.shape[0] // (outer_count * inner_count)
    grid_grad = flat_grad.reshape(outer_count, inner_count, shard_len)
    inner_grad = lax.psum_scatter(
        grid_grad.astype(jnp.bfloat16), "fsdp", scatter_dimension=1, tiled=True
    )
    outer_grad = lax.psum_scatter(inner_grad, "dp", scatter_dimension=0, tiled=True).astype(
        jnp.float32
    )
    shard_grad = outer_grad.reshape(shard_len)
    return (output, grad_tokens.astype(bf16), shard_grad)


def solution(mesh):
    placed = (
        P(("dp", "fsdp"), None),
        P(("dp", "fsdp"), None),
        P(("dp", "fsdp")),
        P(("dp", "fsdp"), None),
    )
    return jax.shard_map(
        shards,
        mesh=mesh,
        in_specs=placed,
        out_specs=(P(("dp", "fsdp"), None), P(("dp", "fsdp"), None), P(("dp", "fsdp"))),
        check_vma=False,
    )
```

profile of v0, /device:TPU:2, one launch (start us, length us, event | category | flops | bytes accessed | tf_op | source)
XLA Modules:
  0.0 1433.8 jit_solution(2873599030516511500)
XLA Ops:
  7.2 4.2 reshape.570
  21.6 4.3 copy.381
  27.3 105.4 %all-gather.3.cloned.1.call-done = bf16[32,1,139520]{2,1,0:T(2,128)(2,1)} async-done(((bf16[1,1,139520]{2,1,0:T(2,128)(2,1)}), bf16[32,1,139520]{2,1,0:T(2,128)(2,1)}) %all-gather.3.cloned.1.call-update) | async-done | bytes 8929296 | tf_op jit(solution)/shard_map/all_gather | solution.py:95
  132.7 187.6 %reduce.3 = bf16[32,139520]{1,0:T(8,128)(2,1)} reduce(bf16[32,1,139520]{2,1,0:T(2,128)(2,1)} %all-gather.3.cloned.1.call-done, bf16[]{:T(256)} %constant.188), dimensions={1}, to_apply=%all-gather.reduce_sub_computation | reduce | bytes 17858562 | tf_op jit(solution)/shard_map/all_gather | solution.py:95
  320.4 16.4 %reshape.571 = bf16[4464640]{0:T(1024)(128)(2,1)} reshape(bf16[32,139520]{1,0:T(8,128)(2,1)} %reduce.3) | data formatting | bytes 17858560
  341.5 5.2 fusion.180
  352.9 6.2 fusion.132
  376.2 23.2 %add_convert_fusion = bf16[3,512,768]{2,1,0:T(8,128)(2,1)S(1)} fusion(f32[3,512,768]{2,1,0:T(8,128)} %bitcast.434, f32[3,512]{1,0:T(4,128)} %get-tuple-element.345, f32[768]{0:T(1024)} %get-tuple-element.336, f32[3,512]{1,0:T(4,128)S(1)} %get-tuple-element.346, f32[768]{0:T(1024)} %get-tuple-element.337, f32[3,512]{1,0:T(4,128)} %get-tuple-element.347, ...), kind=kLoop, calls=%fused_computation.149 | loop fusion | flops 30670848 | bytes 7154688 | tf_op jit(solution)/shard_map/convert_element_type | solution.py:119
  406.9 5.2 mul.975.clone
  412.1 5.7 reshape.576
  418.2 3.8 mul.981.clone
  422.0 5.7 reshape.577
  428.0 4.0 mul.987.clone
  432.0 5.7 reshape.578
  438.0 3.8 mul.993.clone
  441.9 5.7 reshape.579
  447.9 3.8 mul.999.clone
  451.7 5.7 reshape.580
  461.6 5.7 reshape.581
  471.4 5.7 reshape.582
  481.3 5.7 reshape.583
  491.1 5.7 reshape.584
  501.5 8.3 slice_multiply_fusion.7
  554.8 23.3 %while.28 = (s32[]{:T(128)}, bf16[3,512,6,64]{1,3,2,0:T(8,128)(2,1)}, f32[3,6,512,1]{2,1,3,0:T(8,128)}, bf16[3,512,6,64]{1,3,2,0:T(8,128)(2,1)}, s32[3,512]{1,0:...) while((s32[]{:T(128)}, bf16[3,512,6,64]{1,3,2,0:T(8,128)(2,1)}, ...), condition=%wide.region_5.6_spmd.clone, body=%wide.region_2.5_spmd.sunk.clone | while | flops 421786624 | bytes 22000208 | solution.py:160
  578.1 5.0 copy.436
  583.2 5.0 reshape.575
  590.0 14.8 %fusion.120 = bf16[1536,384]{1,0:T(8,128)(2,1)S(1)} fusion(f32[1536,384]{1,0:T(8,128)} %reshape.584, f32[3,512,384]{2,1,0:T(8,128)} %copy.376, f32[1536,384]{1,0:T(8,128)} %reshape.583, f32[3,512,384]{2,1,0:T(8,128)} %copy.372, f32[1536,384]{1,0:T(8,128)} %reshape.582, f32[3,512,384]{2,1,0:T(8,128)} %copy.368, f32[1536,384]{1,0:T(8,128)} %reshape.581, ...), kind=kLoop, calls=%fused_computation.234 | loop fusion | flops 12386304 | bytes 43648512 | tf_op jit(solution)/shard_map/convert.65
  610.7 5.6 reshape.537
  622.0 50.9 %fusion.61 = (bf16[1536,2,1536]{2,0,1:T(8,128)(2,1)}, f32[1536,2,1536]{2,0,1:T(8,128)}, f32[2,1536,1536]{2,1,0:T(8,128)}) fusion(f32[2,1536]{1,0:T(2,128)S(1)} %reshape.566, bf16[1536,2,384]{0,2,1:T(8,128)(2,1)S(1)} %bitcast.454, bf16[2,384,1536]{2,1,0:T(8,128)(2,1)S(1)} %copy-done.40), kind=kOutput, calls=%fused_computation.78 | convolution fusion | flops 3935305728 | bytes 51916800 | tf_op jit(solution)/shard_map/tgi,gio->tgo/dot_general | solution.py:171
  673.0 10.3 fusion.188
  691.3 3.9 fusion.175
  699.7 23.4 %fusion.185 = (bf16[2,1536]{1,0:T(2,128)(2,1)}, bf16[1536,2,1536]{2,0,1:T(8,128)(2,1)}) fusion(f32[1536,2,1536]{2,0,1:T(8,128)} %get-tuple-element.272, bf16[1536,2,384]{0,2,1:T(8,128)(2,1)} %bitcast.452, bf16[2,1536,384]{2,1,0:T(8,128)(2,1)} %reshape.538, f32[2,1536,1536]{2,1,0:T(8,128)} %get-tuple-element.354, f32[2,1536]{1,0:T(2,128)S(1)} %reshape.566), kind=kOutput, calls=%fused_computation.368 | convolution fusion | flops 3699373056 | bytes 51922944 | tf_op jit(solution)/shard_map/tgo,gio->tgi/dot_general | solution.py:196
  723.1 10.5 fusion.86
  733.6 5.1 multiply_reduce_fusion.2
  742.1 4.3 fusion.138
  755.2 10.8 convolution_convert_fusion
  766.0 8.9 fusion.91
  775.0 5.6 convolution_convert_fusion.1
  788.6 4.9 reshape.542
  793.6 4.8 squeeze.48
  798.4 34.5 %fusion.94 = (f32[3,512,6]{1,0,2:T(4,128)S(1)}, f32[3,512,6]{1,0,2:T(4,128)S(1)}, f32[3,512,6]{1,0,2:T(4,128)S(1)}, f32[3,512,6]{1,0,2:T(4,128)S(1)}, f32[3,512,...) fusion(f32[3,512,6,64]{1,0,3,2:T(4,128)} %reshape.542, ...), kind=kLoop, calls=%fused_computation.165 | loop fusion | flops 12303360 | bytes 23926272 | tf_op jit(solution)/shard_map/reduce_sum | solution.py:219
  838.5 4.4 copy.397
  842.9 51.0 %while.29 = (s32[]{:T(128)}, f32[3,512,6,64]{1,3,2,0:T(8,128)}, bf16[3,512,6,64]{1,3,2,0:T(8,128)(2,1)}, f32[3,512,6,64]{1,3,2,0:T(8,128)}, bf16[3,512,6,64]{1,3...) while((s32[]{:T(128)}, f32[3,512,6,64]{1,3,2,0:T(8,128)}, ...), condition=%wide.region_28.29_spmd.clone, body=%wide.region_26.28_spmd.sunk.clone | while | flops 1030878208 | bytes 53443692 | solution.py:298
  893.9 5.5 copy.448
  899.4 5.9 reshape.587
  913.4 13.9 multiply_multiply_fusion.1
  927.4 10.3 multiply_reduce_fusion.3
  941.0 5.6 reshape.558
  953.9 6.1 fusion.172
  961.5 4.3 fusion.181
  979.1 8.6 convert_bitcast_fusion
  987.6 4.4 copy.417
  992.0 5.0 reshape.555
  1005.5 128.5 %concatenate.9 = bf16[4464640]{0:T(1024)(128)(2,1)} concatenate(bf16[1179648]{0:T(1024)(128)(2,1)} %reshape.555, bf16[294912]{0:T(1024)(128)(2,1)} %reshape.556, bf16[589824]{0:T(1024)(128)(2,1)S(1)} %copy-done.32, bf16[1179648]{0:T(1024)(128)(2,1)} %reshape.558, bf16[1179648]{0:T(1024)(128)(2,1)S(1)} %copy-done.25, bf16[6912]{0:T(1024)(128)(2,1)S(1)} %copy-done.114, ...), dimensions={0} | concatenate | bytes 17858560 | tf_op jit(solution)/shard_map/concatenate | solution.py:336
  1134.0 12.5 convert_element_type.302
  1146.5 8.8 copy.421
  1157.2 18.6 %fusion.81 = f32[3,512,768]{2,1,0:T(8,128)} fusion(f32[3,512,768]{2,1,0:T(8,128)} %get-tuple-element.304, f32[3,512,768]{2,1,0:T(8,128)} %get-tuple-element.303, f32[3,512,768]{2,1,0:T(8,128)} %get-tuple-element.302, f32[3,512,768]{2,1,0:T(8,128)} %get-tuple-element.301, f32[3,512,768]{2,1,0:T(8,128)} %get-tuple-element.300, ...), kind=kLoop, calls=%fused_computation.109 | loop fusion | flops 10616832 | bytes 47188992 | tf_op jit(solution)/shard_map/add | solution.py:269
  1175.8 6.1 copy.393
  1181.9 158.5 %all-reduce.24.cloned.1.call-done = bf16[4,8,139520]{2,0,1:T(4,128)(2,1)} async-done(((bf16[4,8,139520]{2,0,1:T(4,128)(2,1)}), bf16[4,8,139520]{2,0,1:T(4,128)(2,1)}) %all-reduce.24.cloned.1.call-update) | async-done | bytes 8929296
  1342.5 5.5 copy.422
  1348.0 8.2 fusion.83
  1356.2 4.4 copy.424
  1363.1 57.1 %all-reduce.26.cloned.1.call-done = bf16[4,1,139520]{2,1,0:T(2,128)(2,1)} async-done(((bf16[4,1,139520]{2,1,0:T(2,128)(2,1)}), bf16[4,1,139520]{2,1,0:T(2,128)(2,1)}) %all-reduce.26.cloned.1.call-update) | async-done | bytes 1116176
  1420.2 7.0 fusion.139
  (505 shorter events, 287.1 us)
Async XLA Ops:
  7.2 125.6 %all-gather.3.cloned.1.call-start = ((), (), s32[]{:S(2)}) async-start(), calls=%async_computation | async-start | bytes 18416640 | tf_op jit(solution)/shard_map/all_gather | solution.py:95
  11.5 1328.9 %all-reduce.24.cloned.1.call-start = ((), (), s32[]{:S(2)}) async-start(), calls=%async_computation.1 | async-start | bytes 17858560
  27.3 474.1 %copy-start.77 = (f32[3,512]{1,0:T(4,128)}, f32[3,512]{1,0:T(4,128)S(1)}, u32[]{:S(2)}) copy-start(f32[3,512]{1,0:T(4,128)S(1)} %get-tuple-element.344) | copy-start | bytes 18436
  27.3 474.1 %copy-start.79 = (f32[3,512]{1,0:T(4,128)}, f32[3,512]{1,0:T(4,128)S(1)}, u32[]{:S(2)}) copy-start(f32[3,512]{1,0:T(4,128)S(1)} %get-tuple-element.346) | copy-start | bytes 18436
  362.0 134.8 %copy-start.12 = (f32[1536,1,384]{2,0,1:T(8,128)}, f32[1536,1,384]{2,0,1:T(8,128)S(1)}, u32[]{:S(2)}) copy-start(f32[1536,1,384]{2,0,1:T(8,128)S(1)} %get-tuple-element.278) | copy-start | bytes 7077892
  364.8 36.1 %copy-start.18 = (bf16[1536,384]{1,0:T(8,128)(2,1)}, bf16[1536,384]{1,0:T(8,128)(2,1)S(1)}, u32[]{:S(2)}) copy-start(bf16[1536,384]{1,0:T(8,128)(2,1)S(1)} %fusion.129) | copy-start | bytes 3538948
  376.2 23.3 %copy-start.58 = (bf16[768,384]{1,0:T(8,128)(2,1)S(1)}, bf16[768,384]{1,0:T(8,128)(2,1)}, u32[]{:S(2)}) copy-start(bf16[768,384]{1,0:T(8,128)(2,1)} %reshape.524) | copy-start | bytes 1769476
  376.2 23.3 %copy-start.138 = (f32[384]{0:T(512)S(1)}, f32[384]{0:T(512)}, u32[]{:S(2)}) copy-start(f32[384]{0:T(512)} %get-tuple-element.291) | copy-start | bytes 4612
  405.6 12.2 copy-start.75
  405.6 12.2 copy-start.73
  405.7 22.1 %copy-start.71 = (f32[3,512,6]{1,0,2:T(4,128)}, f32[3,512,6]{1,0,2:T(4,128)S(1)}, u32[]{:S(2)}) copy-start(f32[3,512,6]{1,0,2:T(4,128)S(1)} %get-tuple-element.332) | copy-start | bytes 110596
  405.7 32.1 %copy-start.69 = (f32[3,512,6]{1,0,2:T(4,128)}, f32[3,512,6]{1,0,2:T(4,128)S(1)}, u32[]{:S(2)}) copy-start(f32[3,512,6]{1,0,2:T(4,128)S(1)} %get-tuple-element.331) | copy-start | bytes 110596
  405.7 41.9 %copy-start.59 = (f32[3,512,6]{1,0,2:T(4,128)}, f32[3,512,6]{1,0,2:T(4,128)S(1)}, u32[]{:S(2)}) copy-start(f32[3,512,6]{1,0,2:T(4,128)S(1)} %get-tuple-element.326) | copy-start | bytes 110596
  405.7 51.8 %copy-start.67 = (f32[3,512,6]{1,0,2:T(4,128)}, f32[3,512,6]{1,0,2:T(4,128)S(1)}, u32[]{:S(2)}) copy-start(f32[3,512,6]{1,0,2:T(4,128)S(1)} %get-tuple-element.330) | copy-start | bytes 110596
  405.7 61.6 %copy-start.65 = (f32[3,512,6]{1,0,2:T(4,128)}, f32[3,512,6]{1,0,2:T(4,128)S(1)}, u32[]{:S(2)}) copy-start(f32[3,512,6]{1,0,2:T(4,128)S(1)} %get-tuple-element.329) | copy-start | bytes 110596
  405.7 71.5 %copy-start.63 = (f32[3,512,6]{1,0,2:T(4,128)}, f32[3,512,6]{1,0,2:T(4,128)S(1)}, u32[]{:S(2)}) copy-start(f32[3,512,6]{1,0,2:T(4,128)S(1)} %get-tuple-element.328) | copy-start | bytes 110596
  405.7 81.3 %copy-start.61 = (f32[3,512,6]{1,0,2:T(4,128)}, f32[3,512,6]{1,0,2:T(4,128)S(1)}, u32[]{:S(2)}) copy-start(f32[3,512,6]{1,0,2:T(4,128)S(1)} %get-tuple-element.327) | copy-start | bytes 110596
  491.1 7.7 copy-start.129
  578.1 11.9 copy-start.4
  578.1 26.8 %copy-start.6 = (bf16[3,512,6,64]{1,3,2,0:T(8,128)(2,1)}, bf16[3,512,6,64]{1,3,2,0:T(8,128)(2,1)S(1)}, u32[]{:S(2)}) copy-start(bf16[3,512,6,64]{1,3,2,0:T(8,128)(2,1)S(1)} %get-tuple-element.573) | copy-start | bytes 3538948
  578.1 10.1 slice-start.4
  578.1 11.9 copy-start.130
  590.0 14.9 %copy-start.27 = (bf16[1536,768]{0,1:T(8,128)(2,1)S(1)}, bf16[1536,768]{0,1:T(8,128)(2,1)}, u32[]{:S(2)}) copy-start(bf16[1536,768]{0,1:T(8,128)(2,1)} %copy-done.26) | copy-start | bytes 7077892
  590.0 14.9 %copy-start.50 = (bf16[768,768]{1,0:T(8,128)(2,1)S(1)}, bf16[768,768]{1,0:T(8,128)(2,1)}, u32[]{:S(2)}) copy-start(bf16[768,768]{1,0:T(8,128)(2,1)} %reshape.535) | copy-start | bytes 3538948
  590.0 14.9 %copy-start.52 = (bf16[1536,384]{1,0:T(8,128)(2,1)S(1)}, bf16[1536,384]{1,0:T(8,128)(2,1)}, u32[]{:S(2)}) copy-start(bf16[1536,384]{1,0:T(8,128)(2,1)} %reshape.575) | copy-start | bytes 3538948
  590.0 14.9 %copy-start.137 = (f32[768]{0:T(1024)S(1)}, f32[768]{0:T(1024)}, u32[]{:S(2)}) copy-start(f32[768]{0:T(1024)} %get-tuple-element.285) | copy-start | bytes 9220
  610.7 8.1 copy-start.110
  610.7 8.1 copy-start.126
  618.7 64.6 %slice-start = ((s8[4718592]{0:T(1024)(128)(4,1)}), s8[4194304]{0:T(1024)(128)(4,1)S(1)}, s32[]{:S(2)}) async-start(s8[4718592]{0:T(1024)(128)(4,1)} %bitcast.432), calls=%async_computation.3 | async-start | bytes 8388608
  622.0 51.0 %copy-start.41 = (bf16[1536,768]{0,1:T(8,128)(2,1)}, bf16[1536,768]{0,1:T(8,128)(2,1)S(1)}, u32[]{:S(2)}) copy-start(bf16[1536,768]{0,1:T(8,128)(2,1)S(1)} %fusion.90) | copy-start | bytes 7077892
  622.0 61.3 %slice-start.1 = ((s8[4718592]{0:T(1024)(128)(4,1)}), s8[524288]{0:T(1024)(128)(4,1)S(1)}, s32[]{:S(2)}) async-start(s8[4718592]{0:T(1024)(128)(4,1)} %bitcast.432), calls=%async_computation.4 | async-start | bytes 1048576
  673.0 10.4 copy-start.135
  723.1 10.5 copy-start.3
  740.0 35.0 %copy-start.127 = (f32[1536]{0:T(1024)}, f32[1536]{0:T(1024)S(1)}, u32[]{:S(2)}) copy-start(f32[1536]{0:T(1024)S(1)} %negate_multiply_fusion.1) | copy-start | bytes 18436
  750.4 35.9 %copy-start.14 = (f32[1536,384]{1,0:T(8,128)}, f32[1536,384]{1,0:T(8,128)S(1)}, u32[]{:S(2)}) copy-start(f32[1536,384]{1,0:T(8,128)S(1)} %slice.462) | copy-start | bytes 7077892
  755.2 10.8 copy-start.42
  766.0 8.9 copy-start.47
  766.0 8.9 copy-start.53
  775.0 7.5 copy-start.70
  775.0 8.2 copy-start.68
  775.0 8.8 copy-start.66
  775.0 9.4 copy-start.64
  775.0 10.0 copy-start.62
  775.0 10.6 copy-start.60
  788.6 9.7 copy-start.9
  798.4 34.7 %copy-start.23 = (f32[3,512,6,9]{1,0,3,2:T(4,128)S(1)}, f32[3,512,6,9]{1,0,3,2:T(4,128)}, u32[]{:S(2)}) copy-start(f32[3,512,6,9]{1,0,3,2:T(4,128)} %copy-done.22) | copy-start | bytes 995332
  798.4 34.8 %copy-start.45 = (f32[3,512,6]{1,0,2:T(4,128)S(1)}, f32[3,512,6]{1,0,2:T(4,128)}, u32[]{:S(2)}) copy-start(f32[3,512,6]{1,0,2:T(4,128)} %copy-done.44) | copy-start | bytes 110596
  834.6 8.3 copy-start.5
  899.4 8.0 copy-start.16
  899.4 8.0 copy-start.19
  911.0 16.3 %slice-start.2 = ((s8[4718592]{0:T(1024)(128)(4,1)}), s8[4194304]{0:T(1024)(128)(4,1)S(1)}, s32[]{:S(2)}) async-start(s8[4718592]{0:T(1024)(128)(4,1)} %bitcast.435), calls=%async_computation.5 | async-start | bytes 8388608
  913.4 13.9 slice-start.3
  913.4 13.9 copy-start.97
  913.4 13.9 copy-start.117
  927.4 10.4 copy-start.1
  927.4 11.1 copy-start.39
  938.5 8.1 copy-start.48
  987.6 17.9 %copy-start.25 = (bf16[1179648]{0:T(1024)(128)(2,1)S(1)}, bf16[1179648]{0:T(1024)(128)(2,1)}, u32[]{:S(2)}) copy-start(bf16[1179648]{0:T(1024)(128)(2,1)} %reshape.559) | copy-start | bytes 7077892
  987.6 17.9 %copy-start.32 = (bf16[589824]{0:T(1024)(128)(2,1)S(1)}, bf16[589824]{0:T(1024)(128)(2,1)}, u32[]{:S(2)}) copy-start(bf16[589824]{0:T(1024)(128)(2,1)} %reshape.557) | copy-start | bytes 3538948
  987.6 17.9 %copy-start.114 = (bf16[6912]{0:T(1024)(128)(2,1)S(1)}, bf16[6912]{0:T(1024)(128)(2,1)}, u32[]{:S(2)}) copy-start(bf16[6912]{0:T(1024)(128)(2,1)} %reshape.560) | copy-start | bytes 41476
  1155.4 264.8 %all-reduce.26.cloned.1.call-start = ((), (), s32[]{:S(2)}) async-start(), calls=%async_computation.2 | async-start | bytes 4464640
  1181.9 166.1 %copy-start.38 = (bf16[4,768,384]{2,1,0:T(8,128)(2,1)S(1)}, bf16[4,768,384]{2,1,0:T(8,128)(2,1)}, u32[]{:S(2)}) copy-start(bf16[4,768,384]{2,1,0:T(8,128)(2,1)} %reshape.520) | copy-start | bytes 7077892
  1181.9 166.2 %copy-start.49 = (bf16[3,512,384]{2,1,0:T(8,128)(2,1)S(1)}, bf16[3,512,384]{2,1,0:T(8,128)(2,1)}, u32[]{:S(2)}) copy-start(bf16[3,512,384]{2,1,0:T(8,128)(2,1)} %copy.412) | copy-start | bytes 3538948
  1181.9 166.2 %copy-start.128 = (f32[1536]{0:T(1024)S(1)}, f32[1536]{0:T(1024)}, u32[]{:S(2)}) copy-start(f32[1536]{0:T(1024)} %copy-done.127) | copy-start | bytes 18436
  (86 other events, 272.4 us)
Sparse Core Ops, SparseCore 0:
  11.6 121.1 all-gather.2
  1155.5 184.7 all-reduce.23
  1348.1 71.9 all-reduce.25
where the time goes:
time: 1460 us; the launch traced here: 1430 us
  local copies, waits for them, and re-layouts  498 us (34%)
  other arithmetic  371 us (25%)
  waiting for transfers between devices  321 us (22%)
  matrix products  227 us (16%)
  between operations  15.7 us (1%)
    unnamed x5, waiting for transfers between devices  216 us
    all_gather x1, other arithmetic, shards(): gathered = lax.all_gather(params, ('dp', 'fsdp'), axis=0, tiled=True)  188 us
    concatenate x1, local copies, waits for them, and re-layouts, shards(): jnp.concatenate(pieces + [jnp.zeros((gathered.shape[0] - used_size,), f32)])  128 us
    all_gather x1, waiting for transfers between devices, shards(): gathered = lax.all_gather(params, ('dp', 'fsdp'), axis=0, tiled=True)  105 us
    mul x28, local copies, waits for them, and re-layouts, shards(): tap_weights[..., tap_index:tap_index + 1]  93.2 us
    unnamed x323, local copies, waits for them, and re-layouts  60.5 us
    dot_general x1, matrix products, shards(): jnp.einsum('tgi,gio->tgo', normed_low, weights['ffn_in'], preferred_eleme...  50.9 us
    reduce_sum x1, other arithmetic, shards(): jnp.sum(grad_conv_out * (shift_rows(conv32, tap_index - half_taps) * tap_...  34.5 us
  transfers between devices with their start and end apart: 3, of which 3 were waited for; matrix products, arithmetic and copies ran while one was open for 4% of the time, Pallas kernels for 0%

commit v1 on v0

v1 whole, which is shorter than its diff:
```python
import math

import jax
import jax.numpy as jnp
from jax import lax
from jax.experimental import pallas as pl
from jax.experimental.pallas import tpu as pltpu
from jax.sharding import PartitionSpec as P

D = 768
HEADS = 6
HEAD_DIM = 64
ATT = HEADS * HEAD_DIM
FF = 3072
GROUPS = 2
KS = 9
HALF = KS // 2
SLOTS = 16
EPS = 1e-12
LANES = 128
NEG = -1e30
BIG = 3e38
SCALE = HEAD_DIM ** (-0.5)

f32 = jnp.float32
bf16 = jnp.bfloat16
i32 = jnp.int32

PIECES = [
    ("proj", 4 * D, ATT),
    ("point", D, ATT),
    ("dense", D, D),
    ("ffn_in", D, FF // GROUPS),
    ("ffn_out", FF, D // GROUPS),
]
START = {}
_at = 0
for _name, _r, _c in PIECES:
    START[_name] = _at
    _at += _r * _c // LANES
START["depth"] = _at
START["kernel"] = _at + KS * D // LANES
START["bias4"] = START["kernel"] + ATT * HEADS * KS // LANES
START["tail"] = START["bias4"] + 4 * ATT // LANES
USED = START["tail"] + 61
KB = HEADS * KS

QB, VB, CB, PB, KBR, DB, N1G, N1S, FIB, FOB, N2G, N2S, DW = range(13)
VROWS = 24
TAIL = [(DB, 6), (N1G, 6), (N1S, 6), (FIB, 24), (FOB, 6), (N2G, 6), (N2S, 6)]

VM = pltpu.VMEM
VMEM_LIMIT = 62 * 1024 * 1024


def nn(a, b):
    return lax.dot_general(a, b, (((1,), (0,)), ((), ())), preferred_element_type=f32)


def nt(a, b):
    return lax.dot_general(a, b, (((1,), (1,)), ((), ())), preferred_element_type=f32)


def tn(a, b):
    return lax.dot_general(a, b, (((0,), (0,)), ((), ())), preferred_element_type=f32)


def iota(shape, axis):
    return lax.broadcasted_iota(i32, shape, axis)


def loop(count, body, unroll=1):
    def step(i, carry):
        body(i)
        return carry

    lax.fori_loop(0, count, step, 0, unroll=unroll)


def tap_perm():
    k, n = iota((LANES, LANES), 0), iota((LANES, LANES), 1)
    head, tap = n & 7, n >> 3
    return jnp.where((k == head * KS + tap) & (head < HEADS) & (tap < KS), 1.0, 0.0).astype(bf16)


def used_taps(shape):
    n = iota(shape, len(shape) - 1)
    return ((n & 7) < HEADS) & ((n >> 3) < KS)


def padded(rows):
    return -(-rows // 16) * 16


def unpack_kernel(count, rows, g_ref, wp_ref, pw_ref, dw_ref, fi_ref, fo_ref, kw_ref, vec_ref, flat, kwt):
    pad = padded(rows)

    def spread(i):
        flat[pl.ds(i * rows, pad), :] = g_ref[i].astype(f32)

    for i in range(count):
        spread(i)

    def piece(name, out, height, width, row0, col0, skip):
        per = width // LANES
        base = START[name] + skip
        for c in range(per):
            for r in range(0, height, 256):
                part = min(256, height - r)
                out[row0 + r : row0 + r + part, col0 + c * LANES : col0 + (c + 1) * LANES] = flat[
                    pl.ds(base + r * per + c, part, stride=per), :
                ].astype(bf16)

    for m in range(4):
        piece("proj", wp_ref, D, ATT, 0, m * ATT, m * D * ATT // LANES)
    piece("point", pw_ref, D, ATT, 0, 0, 0)
    piece("dense", dw_ref, D, D, 0, 0, 0)
    piece("ffn_in", fi_ref, D, FF // GROUPS, 0, 0, 0)
    piece("ffn_out", fo_ref, FF, D // GROUPS, 0, 0, 0)

    vec_ref[...] = jnp.zeros_like(vec_ref)
    for row in range(4):
        for c in range(3):
            at = START["bias4"] + row * 3 + c
            vec_ref[row : row + 1, c * LANES : (c + 1) * LANES] = flat[at : at + 1, :]
    for j in range(KS):
        for c in range(6):
            at = START["depth"] + j * 6 + c
            vec_ref[DW + j : DW + j + 1, c * LANES : (c + 1) * LANES] = flat[at : at + 1, :]
    at = START["tail"]
    lane = iota((64, LANES), 1)
    first = pltpu.roll(flat[at : at + 64, :], LANES - KB, 1)
    second = pltpu.roll(flat[at + 1 : at + 65, :], LANES - KB, 1)
    kwt[0:64, :] = jnp.where(lane < LANES - KB, first, second)
    at = 0
    for row, many in TAIL:
        for c in range(many):
            vec_ref[row : row + 1, c * LANES : (c + 1) * LANES] = kwt[at + c : at + c + 1, :]
        at += many
    perm = tap_perm()
    lane8 = iota((16, LANES), 1)
    kb = jnp.broadcast_to(flat[START["tail"] : START["tail"] + 1, :], (16, LANES))
    kb = nn(jnp.where(lane8 < KB, kb, 0.0).astype(bf16), perm)
    kb = jnp.where(used_taps((16, LANES)), kb, NEG)
    vec_ref[KBR : KBR + 1, 0:LANES] = kb[0:1]

    lane = iota((8, LANES), 1)
    for a in range(64):
        c0, ln = divmod(a * KB, LANES)
        at = START["kernel"] + c0
        x = pltpu.roll(flat[pl.ds(at, 8, stride=27), :], (LANES - ln) % LANES, 1)
        if ln + KB > LANES:
            y = pltpu.roll(flat[pl.ds(at + 1, 8, stride=27), :], (LANES - ln) % LANES, 1)
            x = jnp.where(lane < LANES - ln, x, y)
        kwt[pl.ds(a, 8, stride=64), :] = jnp.where(lane < KB, x, 0.0)
    kw_ref[...] = nn(kwt[0:ATT, :].astype(bf16), perm).astype(bf16)


def flat_rows(count, rows):
    return -(-(max((count - 1) * rows + padded(rows), USED + 240)) // 8) * 8


def run_unpack(gathered, rows):
    count = gathered.shape[0]
    shapes = [(D, 4 * ATT), (D, ATT), (D, D), (D, FF // GROUPS), (FF, D // GROUPS), (ATT, LANES)]
    out = [jax.ShapeDtypeStruct(s, bf16) for s in shapes] + [jax.ShapeDtypeStruct((VROWS, FF), f32)]

    def body(*refs):
        unpack_kernel(count, rows, *refs)

    return pl.pallas_call(
        body,
        out_shape=out,
        in_specs=[pl.BlockSpec(memory_space=VM)],
        out_specs=[pl.BlockSpec(memory_space=VM)] * len(out),
        scratch_shapes=[VM((flat_rows(count, rows), LANES), f32), VM((512, LANES), f32)],
        compiler_params=pltpu.CompilerParams(vmem_limit_bytes=VMEM_LIMIT),
        name="unpack",
    )(gathered)


def pack_kernel(count, rows, gp_ref, gpw_ref, gdw_ref, gfi_ref, gfo_ref, gkw_ref, va_ref, vb_ref, send_ref, flat, kwt, vec):
    total = flat.shape[0]
    used8 = START["depth"] // 8 * 8
    flat[used8:total, :] = jnp.zeros((total - used8, LANES), f32)
    vec[...] = va_ref[...] + vb_ref[...]

    def piece(name, src, height, width, row0, col0, skip):
        per = width // LANES
        base = START[name] + skip
        for c in range(per):
            for r in range(0, height, 256):
                part = min(256, height - r)
                flat[pl.ds(base + r * per + c, part, stride=per), :] = src[
                    row0 + r : row0 + r + part, col0 + c * LANES : col0 + (c + 1) * LANES
                ]

    for m in range(4):
        piece("proj", gp_ref, D, ATT, 0, m * ATT, m * D * ATT // LANES)
    piece("point", gpw_ref, D, ATT, 0, 0, 0)
    piece("dense", gdw_ref, D, D, 0, 0, 0)
    piece("ffn_in", gfi_ref, D, FF // GROUPS, 0, 0, 0)
    piece("ffn_out", gfo_ref, FF, D // GROUPS, 0, 0, 0)

    perm = tap_perm()
    kwt[...] = jnp.zeros_like(kwt)
    kwt[0:ATT, :] = nt(gkw_ref[...].astype(bf16), perm)
    lane = iota((8, LANES), 1)
    for a in range(64):
        c0, ln = divmod(a * KB, LANES)
        at = START["kernel"] + c0
        x = pltpu.roll(kwt[pl.ds(a, 8, stride=64), :], ln, 1)
        if ln + KB > LANES:
            flat[pl.ds(at, 8, stride=27), :] += jnp.where(lane >= ln, x, 0.0)
            flat[pl.ds(at + 1, 8, stride=27), :] += jnp.where(lane < ln, x, 0.0)
        else:
            flat[pl.ds(at, 8, stride=27), :] += x
    for row in range(4):
        for c in range(3):
            at = START["bias4"] + row * 3 + c
            flat[at : at + 1, :] = vec[row : row + 1, c * LANES : (c + 1) * LANES]
    for j in range(KS):
        for c in range(6):
            at = START["depth"] + j * 6 + c
            flat[at : at + 1, :] = vec[DW + j : DW + j + 1, c * LANES : (c + 1) * LANES]
    kwt[...] = jnp.zeros_like(kwt)
    at = 8
    for row, many in TAIL:
        for c in range(many):
            kwt[at + c : at + c + 1, :] = vec[row : row + 1, c * LANES : (c + 1) * LANES]
        at += many
    lane = iota((72, LANES), 1)
    before = pltpu.roll(kwt[7:79, :], KB, 1)
    here = pltpu.roll(kwt[8:80, :], KB, 1)
    at = START["tail"]
    flat[at : at + 72, :] = jnp.where(lane < KB, before, here)
    kb = jnp.broadcast_to(vec[KBR : KBR + 1, 0:LANES], (16, LANES))
    kb = nt(jnp.where(used_taps((16, LANES)), kb, 0.0).astype(bf16), perm)
    lane = iota((1, LANES), 1)
    flat[at : at + 1, :] = jnp.where(lane < KB, kb[0:1], flat[at : at + 1, :])

    pad = padded(rows)
    for i in range(count):
        send_ref[i] = flat[i * rows : i * rows + pad, :].astype(bf16)


def run_pack(count, rows, gp, gpw, gdw, gfi, gfo, gkw, va, vb):
    def body(*refs):
        pack_kernel(count, rows, *refs)

    return pl.pallas_call(
        body,
        out_shape=jax.ShapeDtypeStruct((count, padded(rows), LANES), bf16),
        in_specs=[pl.BlockSpec(memory_space=VM)] * 8,
        out_specs=pl.BlockSpec(memory_space=VM),
        scratch_shapes=[
            VM((flat_rows(count, rows), LANES), f32),
            VM((512, LANES), f32),
            VM((VROWS, FF), f32),
        ],
        compiler_params=pltpu.CompilerParams(vmem_limit_bytes=VMEM_LIMIT),
        name="pack",
    )(gp, gpw, gdw, gfi, gfo, gkw, va, vb)


def doc_marks(r, length, len_ref, dcol, tm, mb):
    t = iota((length, LANES), 0)
    u = iota((8, length), 1)
    ends = jnp.int32(0)
    d = jnp.zeros((length, LANES), i32)
    e = jnp.zeros((8, length), i32)
    for j in range(SLOTS):
        ends = ends + len_ref[r, j]
        d = d + (t >= ends).astype(i32)
        e = e + (u >= ends).astype(i32)
    dcol[0:8, :] = jnp.full((8, LANES), -1, i32)
    dcol[8 : 8 + length, :] = d
    dcol[8 + length : 16 + length, :] = jnp.full((8, LANES), -1, i32)
    for j in range(KS):
        at = 8 + j - HALF
        tm[j] = (dcol[at : at + length, :] == d).astype(f32)
    for c in range(length // LANES):
        mb[:, c * LANES : (c + 1) * LANES] = jnp.where(d == e[0:1, c * LANES : (c + 1) * LANES], BIG, NEG)


def tap_lanes(tm, length):
    tap = iota((length, LANES), 1) >> 3
    out = jnp.zeros((length, LANES), f32)
    for j in range(KS):
        out = jnp.where(tap == j, tm[j], out)
    return jnp.where(used_taps((length, LANES)), out, 0.0)


def over_taps(x, op):
    for s in (8, 16, 32, 64):
        x = op(x, pltpu.roll(x, s, 1))
    return x


def fill_emat(emat):
    k, c = iota((2 * LANES, ATT), 0) & (LANES - 1), iota((2 * LANES, ATT), 1)
    for j in range(KS):
        emat[:, j * ATT : (j + 1) * ATT] = jnp.where(k == j * 8 + (c >> 6), 1.0, 0.0).astype(bf16)


def two_parts(x):
    high = x.astype(bf16)
    return jnp.concatenate([high, (x - high.astype(f32)).astype(bf16)], axis=1)


def zero_pads(ref, length):
    for c in range(ref.shape[0]):
        ref[c, 0:8, :] = jnp.zeros((8, LANES), f32)
        ref[c, 8 + length : 16 + length, :] = jnp.zeros((8, LANES), f32)


def fwd_kernel(length, len_ref, tok_ref, wp_ref, pw_ref, kw_ref, vec_ref,
               qkvc_ref, kc_ref, dep_ref, ca_ref, tap_ref, join_ref, lse_ref,
               xs, cs, dcol, tm, mb, emat, acc):
    row = pl.program_id(0)

    @pl.when(row == 0)
    def _():
        fill_emat(emat)

    doc_marks(row, length, len_ref, dcol, tm, mb)
    tok = tok_ref[...]
    zero_pads(xs, length)
    zero_pads(cs, length)
    for c in range(6):
        xs[c, 8 : 8 + length, :] = tok[:, c * LANES : (c + 1) * LANES].astype(f32)
    for m, bias in ((0, QB), (1, None), (2, VB), (3, CB)):
        x = nn(tok, wp_ref[:, m * ATT : (m + 1) * ATT])
        if bias is not None:
            x = x + vec_ref[bias : bias + 1, 0:ATT]
        x = x.astype(bf16)
        qkvc_ref[:, m * ATT : (m + 1) * ATT] = x
        if m == 3:
            for c in range(3):
                cs[c, 8 : 8 + length, :] = x[:, c * LANES : (c + 1) * LANES].astype(f32)

    step = 64

    for c in range(6):
        w = [vec_ref[DW + j : DW + j + 1, c * LANES : (c + 1) * LANES] for j in range(KS)]
        for r in range(0, length, step):
            total = w[HALF] * xs[c, 8 + r : 8 + r + step, :]
            for j in range(KS):
                if j != HALF:
                    at = 8 + r + j - HALF
                    total = total + w[j] * (xs[c, at : at + step, :] * tm[j, r : r + step, :])
            dep_ref[r : r + step, c * LANES : (c + 1) * LANES] = total.astype(bf16)

    keyconv = nn(dep_ref[...], pw_ref[...]) + vec_ref[PB : PB + 1, 0:ATT]
    kc_ref[...] = keyconv.astype(bf16)
    ca = (keyconv * qkvc_ref[:, 0:ATT].astype(f32)).astype(bf16)
    ca_ref[...] = ca
    logits = nn(ca, kw_ref[...]) + vec_ref[KBR : KBR + 1, 0:LANES]
    e = jnp.exp(logits - over_taps(logits, jnp.maximum))
    taps = e / over_taps(e, jnp.add)
    tap_ref[...] = taps
    spread = two_parts(taps * tap_lanes(tm, length))
    for j in range(KS):
        t = nn(spread, emat[:, j * ATT : (j + 1) * ATT])
        for c in range(3):
            at = 8 + j - HALF
            part = t[:, c * LANES : (c + 1) * LANES] * cs[c, at : at + length, :]
            if j:
                part = part + acc[:, c * LANES : (c + 1) * LANES]
            if j < KS - 1:
                acc[:, c * LANES : (c + 1) * LANES] = part
            else:
                join_ref[:, ATT + c * LANES : ATT + (c + 1) * LANES] = part.astype(bf16)

    for p in range(3):
        cols = slice(p * LANES, (p + 1) * LANES)
        q, k, v = (qkvc_ref[:, m * ATT + p * LANES : m * ATT + (p + 1) * LANES] for m in range(3))
        qs = q.astype(f32) * SCALE
        vt = v.astype(f32).T
        lane, sub = iota((length, LANES), 1), iota((LANES, length), 0)
        halves = []
        for h in range(2):
            qh = jnp.where((lane >= HEAD_DIM) == bool(h), qs, 0.0).astype(bf16)
            vh = jnp.where((sub >= HEAD_DIM) == bool(h), vt, 1.0).astype(bf16)
            z = jnp.minimum(nt(k, qh), mb[...])
            top = jnp.max(z, axis=0, keepdims=True)
            o = nn(vh, jnp.exp(z - top).astype(bf16))
            s = o[(1 - h) * HEAD_DIM : (1 - h) * HEAD_DIM + 1, :]
            lse_ref[0, 2 * p + h : 2 * p + h + 1, :] = top + jnp.log(s)
            halves.append(o[h * HEAD_DIM : (h + 1) * HEAD_DIM, :] / s)
        join_ref[:, cols] = jnp.concatenate(halves, axis=0).T.astype(bf16)


def blocked(rows, cols):
    return pl.BlockSpec((rows, cols), lambda r: (r, 0))


def row_scratch(length):
    return [
        VM((6, length + 16, LANES), f32),
        VM((3, length + 16, LANES), f32),
        VM((length + 16, LANES), i32),
        VM((KS, length, LANES), f32),
        VM((length, length), f32),
        VM((2 * LANES, KS * ATT), bf16),
    ]


def run_fwd(tokens, lengths, wp, pw, kw, vec):
    rows, count = lengths.shape[0], tokens.shape[0]
    length = count // rows

    def body(*refs):
        fwd_kernel(length, *refs)

    full = pl.BlockSpec(memory_space=VM)
    return pl.pallas_call(
        body,
        grid=(rows,),
        out_shape=[
            jax.ShapeDtypeStruct((count, 4 * ATT), bf16),
            jax.ShapeDtypeStruct((count, ATT), bf16),
            jax.ShapeDtypeStruct((count, D), bf16),
            jax.ShapeDtypeStruct((count, ATT), bf16),
            jax.ShapeDtypeStruct((count, LANES), f32),
            jax.ShapeDtypeStruct((count, D), bf16),
            jax.ShapeDtypeStruct((rows, 8, length), f32),
        ],
        in_specs=[pl.BlockSpec(memory_space=pltpu.SMEM), blocked(length, D), full, full, full, full],
        out_specs=[
            blocked(length, 4 * ATT),
            blocked(length, ATT),
            blocked(length, D),
            blocked(length, ATT),
            blocked(length, LANES),
            blocked(length, D),
            pl.BlockSpec((1, 8, length), lambda r: (r, 0, 0)),
        ],
        scratch_shapes=row_scratch(length) + [VM((length, ATT), f32)],
        compiler_params=pltpu.CompilerParams(vmem_limit_bytes=VMEM_LIMIT),
        name="row_forward",
    )(lengths, tokens, wp, pw, kw, vec)


def mid_kernel(length, len_ref, tok_ref, join_ref, cot_ref, dw_ref, fi_ref, fo_ref, vec_ref,
               out_ref, gf_ref, gj_ref, gdw_ref, gfi_ref, gfo_ref, gv_ref,
               xh1, rs1, nl, act, slope, gsec, gsl):
    row = pl.program_id(0)
    fg, dg = FF // GROUPS, D // GROUPS

    @pl.when(row == 0)
    def _():
        for ref in (gdw_ref, gfi_ref, gfo_ref, gv_ref):
            ref[...] = jnp.zeros_like(ref)

    used = jnp.int32(0)
    for j in range(SLOTS):
        used = used + len_ref[row, j]

    def vec(r, n=D):
        return vec_ref[r : r + 1, 0:n]

    step = 64
    gsec[...] = nn(join_ref[...], dw_ref[...])

    def norm1(i):
        at = pl.ds(pl.multiple_of(i * step, step), step)
        z = gsec[at, :] + vec(DB) + tok_ref[at, :].astype(f32)
        z = z - jnp.mean(z, axis=1, keepdims=True)
        r = lax.rsqrt(jnp.mean(z * z, axis=1, keepdims=True) + EPS)
        x = z * r
        xh1[at, :] = x
        rs1[at, :] = jnp.broadcast_to(r, (step, LANES))
        nl[at, :] = (x * vec(N1G) + vec(N1S)).astype(bf16)

    loop(length // step, norm1)

    tile = 512
    per = fg // tile

    for g in range(GROUPS):
        def widen(i, g=g):
            col = pl.ds(pl.multiple_of(i * tile, tile), tile)
            col2 = pl.ds(pl.multiple_of(g * fg + i * tile, tile), tile)
            x = nn(nl[:, g * dg : (g + 1) * dg], fi_ref[g * dg : (g + 1) * dg, col]) + vec_ref[FIB : FIB + 1, col2]
            e = jnp.exp(x * x * -0.5)
            t = pl.reciprocal(1.0 + 0.2316419 * jnp.abs(x), approx=True)
            poly = t * 0.53070271450 - 0.72657601350
            poly = poly * t + 0.71070687050
            poly = poly * t - 0.14224836800
            poly = poly * t + 0.12741479600
            q = poly * t * e
            phi = jnp.where(x >= 0, 1.0 - q, q)
            act[:, col2] = (x * phi).astype(bf16)
            slope[:, col2] = (phi + x * 0.3989422804014327 * e).astype(bf16)

        loop(per, widen)

    for g in range(GROUPS):
        gsec[:, g * dg : (g + 1) * dg] = nn(act[:, g * fg : (g + 1) * fg], fo_ref[g * fg : (g + 1) * fg, :])

    def rows8(x):
        total = x[0:8]
        for k in range(8, x.shape[0], 8):
            total = total + x[k : k + 8]
        return total

    def norm2(i, carry):
        at = pl.ds(pl.multiple_of(i * step, step), step)
        norm = xh1[at, :] * vec(N1G) + vec(N1S)
        z = gsec[at, :] + vec(FOB) + norm
        z = z - jnp.mean(z, axis=1, keepdims=True)
        r = lax.rsqrt(jnp.mean(z * z, axis=1, keepdims=True) + EPS)
        x = z * r
        keep = ((iota((step, 1), 0) + i * step) < used).astype(f32)
        out_ref[at, :] = ((x * vec(N2G) + vec(N2S)) * keep).astype(bf16)
        gf = cot_ref[at, :].astype(f32) * keep
        gx = gf * x
        e = gf * vec(N2G)
        gz = r * (e - jnp.mean(e, axis=1, keepdims=True) - x * jnp.mean(e * x, axis=1, keepdims=True))
        gsec[at, :] = gz
        gsl[at, :] = gz.astype(bf16)
        return (carry[0] + rows8(gx), carry[1] + rows8(gf), carry[2] + rows8(gz))

    none = jnp.zeros((8, D), f32)
    sums = lax.fori_loop(0, length // step, norm2, (none, none, none))

    def add(r, value):
        gv_ref[r : r + 1, 0 : value.shape[1]] += jnp.sum(value, axis=0, keepdims=True)

    for r, value in zip((N2G, N2S, FOB), sums):
        add(r, value)

    for g in range(GROUPS):
        def narrow(i, g=g):
            r0 = pl.ds(pl.multiple_of(g * fg + i * tile, tile), tile)
            x = nt(gsl[:, g * dg : (g + 1) * dg], fo_ref[r0, :]) * slope[:, r0].astype(f32)
            gv_ref[FIB : FIB + 1, r0] += jnp.sum(x, axis=0, keepdims=True)
            slope[:, r0] = x.astype(bf16)
            gfo_ref[r0, :] += tn(act[:, r0], gsl[:, g * dg : (g + 1) * dg])
            col = pl.ds(pl.multiple_of(i * tile, tile), tile)
            gfi_ref[g * dg : (g + 1) * dg, col] += tn(nl[:, g * dg : (g + 1) * dg], slope[:, r0])

        loop(per, narrow)
    for g in range(GROUPS):
        gsec[:, g * dg : (g + 1) * dg] += nt(slope[:, g * fg : (g + 1) * fg], fi_ref[g * dg : (g + 1) * dg, :])

    def norm1_back(i, carry):
        at = pl.ds(pl.multiple_of(i * step, step), step)
        gn = gsec[at, :]
        x = xh1[at, :]
        e = gn * vec(N1G)
        r = rs1[at, :]
        r = jnp.concatenate([r] * (D // LANES), axis=1)
        gz = r * (e - jnp.mean(e, axis=1, keepdims=True) - x * jnp.mean(e * x, axis=1, keepdims=True))
        gf_ref[at, :] = gz.astype(bf16)
        return (carry[0] + rows8(gn * x), carry[1] + rows8(gn), carry[2] + rows8(gz))

    sums = lax.fori_loop(0, length // step, norm1_back, (none, none, none))
    for r, value in zip((N1G, N1S, DB), sums):
        add(r, value)
    low = gf_ref[...]
    gj_ref[...] = nt(low, dw_ref[...]).astype(bf16)
    gdw_ref[...] += tn(join_ref[...], low)


def run_mid(tokens, lengths, joined, cotangent, dw, fi, fo, vec):
    rows, count = lengths.shape[0], tokens.shape[0]
    length = count // rows

    def body(*refs):
        mid_kernel(length, *refs)

    full = pl.BlockSpec(memory_space=VM)
    return pl.pallas_call(
        body,
        grid=(rows,),
        out_shape=[
            jax.ShapeDtypeStruct((count, D), bf16),
            jax.ShapeDtypeStruct((count, D), bf16),
            jax.ShapeDtypeStruct((count, D), bf16),
            jax.ShapeDtypeStruct((D, D), f32),
            jax.ShapeDtypeStruct((D, FF // GROUPS), f32),
            jax.ShapeDtypeStruct((FF, D // GROUPS), f32),
            jax.ShapeDtypeStruct((VROWS, FF), f32),
        ],
        in_specs=[pl.BlockSpec(memory_space=pltpu.SMEM)] + [blocked(length, D)] * 3 + [full] * 4,
        out_specs=[blocked(length, D)] * 3 + [full] * 4,
        scratch_shapes=[
            VM((length, D), f32),
            VM((length, LANES), f32),
            VM((length, D), bf16),
            VM((length, FF), bf16),
            VM((length, FF), bf16),
            VM((length, D), f32),
            VM((length, D), bf16),
        ],
        compiler_params=pltpu.CompilerParams(vmem_limit_bytes=VMEM_LIMIT),
        name="mid",
    )(lengths, tokens, joined, cotangent, dw, fi, fo, vec)


def bwd_kernel(length, len_ref, tok_ref, qkvc_ref, kc_ref, dep_ref, ca_ref, tap_ref, join_ref, lse_ref, gf_ref, gj_ref,
               wp_ref, pw_ref, kw_ref, vec_ref,
               gt_ref, gp_ref, gpw_ref, gkw_ref, gv_ref,
               ds, cs, dcol, tm, mb, emat, gs, tp, prod, gq, gfour, acc):
    row = pl.program_id(0)

    @pl.when(row == 0)
    def _():
        fill_emat(emat)
        for ref in (gp_ref, gpw_ref, gkw_ref, gv_ref):
            ref[...] = jnp.zeros_like(ref)

    doc_marks(row, length, len_ref, dcol, tm, mb)
    for ref in (ds, cs, gs, tp):
        zero_pads(ref, length)

    def add(r, value):
        gv_ref[r : r + 1, 0 : value.shape[1]] += jnp.sum(value, axis=0, keepdims=True)

    for p in range(3):
        cols = slice(p * LANES, (p + 1) * LANES)
        q, k, v = (qkvc_ref[:, m * ATT + p * LANES : m * ATT + (p + 1) * LANES] for m in range(3))
        g = gj_ref[:, cols]
        lane, sub = iota((length, LANES), 1), iota((16, LANES), 1)
        which = iota((16, LANES), 0)
        marks = jnp.where((sub >= HEAD_DIM) == (which >= 8), 1.0, 0.0).astype(bf16)
        dots = g.astype(f32) * join_ref[:, cols].astype(f32)
        high = dots.astype(bf16)
        dots = nt(marks, high) + nt(marks, (dots - high.astype(f32)).astype(bf16))
        qs = q.astype(f32) * SCALE
        kt = k.astype(f32).T.astype(bf16)
        gk, gv, gqt = None, None, []
        for h in range(2):
            own = (lane >= HEAD_DIM) == bool(h)
            qh = jnp.where(own, qs, 0.0).astype(bf16)
            gh = jnp.where(own, g.astype(f32), 0.0).astype(bf16)
            prob = jnp.exp(jnp.minimum(nt(k, qh), mb[...]) - lse_ref[0, 2 * p + h : 2 * p + h + 1, :])
            dsc = (prob * (nt(v, gh) - dots[8 * h : 8 * h + 1, :])).astype(bf16)
            a, b = nn(prob.astype(bf16), gh), nn(dsc, qh)
            gv, gk = (a, b) if h == 0 else (gv + a, gk + b)
            gqt.append(nn(kt, dsc)[h * HEAD_DIM : (h + 1) * HEAD_DIM, :])
        gq[:, cols] = jnp.concatenate(gqt, axis=0).T * SCALE
        gfour[:, ATT + p * LANES : ATT + (p + 1) * LANES] = gk.astype(bf16)
        gfour[:, 2 * ATT + p * LANES : 2 * ATT + (p + 1) * LANES] = gv.astype(bf16)
        gv_ref[VB : VB + 1, cols] += jnp.sum(gv, axis=0, keepdims=True)

    for c in range(3):
        cs[c, 8 : 8 + length, :] = qkvc_ref[:, 3 * ATT + c * LANES : 3 * ATT + (c + 1) * LANES].astype(f32)
        gs[c, 8 : 8 + length, :] = gj_ref[:, ATT + c * LANES : ATT + (c + 1) * LANES].astype(f32)
    for j in range(KS):
        for c in range(3):
            at = 8 + j - HALF
            prod[:, j * ATT + c * LANES : j * ATT + (c + 1) * LANES] = (
                gs[c, 8 : 8 + length, :] * cs[c, at : at + length, :]
            ).astype(bf16)
    marks = tap_lanes(tm, length)
    gtaps = nt(prod[...], emat[0:LANES, :]) * marks
    taps = jnp.where(used_taps((length, LANES)), tap_ref[...], 0.0)
    glog = taps * (gtaps - over_taps(taps * gtaps, jnp.add))
    add(KBR, glog)
    glog = glog.astype(bf16)
    gkw_ref[...] += tn(ca_ref[...], glog)
    gca = nt(glog, kw_ref[...])

    tp[0, 8 : 8 + length, :] = taps * marks
    tap = iota((length, LANES), 1) >> 3
    moved = jnp.zeros((length, LANES), f32)
    for j in range(KS):
        at = 8 + HALF - j
        moved = jnp.where(tap == j, tp[0, at : at + length, :], moved)
    spread = two_parts(moved)
    for j in range(KS):
        t = nn(spread, emat[:, j * ATT : (j + 1) * ATT])
        for c in range(3):
            at = 8 + HALF - j
            part = t[:, c * LANES : (c + 1) * LANES] * gs[c, at : at + length, :]
            if j:
                part = part + acc[:, c * LANES : (c + 1) * LANES]
            if j < KS - 1:
                acc[:, c * LANES : (c + 1) * LANES] = part
            else:
                gfour[:, 3 * ATT + c * LANES : 3 * ATT + (c + 1) * LANES] = part.astype(bf16)
                gv_ref[CB : CB + 1, c * LANES : (c + 1) * LANES] += jnp.sum(part, axis=0, keepdims=True)

    gkc = gca * qkvc_ref[:, 0:ATT].astype(f32)
    gquery = gq[...] + gca * kc_ref[...].astype(f32)
    add(QB, gquery)
    gfour[:, 0:ATT] = gquery.astype(bf16)
    add(PB, gkc)
    gkc = gkc.astype(bf16)
    gpw_ref[...] += tn(dep_ref[...], gkc)
    for c in range(3):
        x = nt(gkc, pw_ref[c * 256 : (c + 1) * 256, :])
        ds[2 * c, 8 : 8 + length, :] = x[:, 0:LANES]
        ds[2 * c + 1, 8 : 8 + length, :] = x[:, LANES:]
    for m in range(4):
        gp_ref[:, m * ATT : (m + 1) * ATT] += tn(tok_ref[...], gfour[:, m * ATT : (m + 1) * ATT])

    step = 64
    for c in range(6):
        cols = slice(c * LANES, (c + 1) * LANES)
        w = [vec_ref[DW + j : DW + j + 1, cols] for j in range(KS)]
        sums = [None] * KS
        if c % 2 == 0:
            direct = nt(gfour[...], wp_ref[c * LANES : (c + 2) * LANES, :])
        for r in range(0, length, step):
            tok = tok_ref[r : r + step, cols].astype(f32)
            total = gf_ref[r : r + step, cols].astype(f32) + direct[r : r + step, (c % 2) * LANES : (c % 2 + 1) * LANES]
            for j in range(KS):
                at = 8 + r + j - HALF
                u = ds[c, at : at + step, :]
                if j != HALF:
                    u = u * tm[j, r : r + step, :]
                total = total + w[KS - 1 - j] * u
                u = tok * u
                part = u[0:8]
                for s in range(8, step, 8):
                    part = part + u[s : s + 8]
                sums[j] = part if r == 0 else sums[j] + part
            gt_ref[r : r + step, cols] = total.astype(bf16)
        for j in range(KS):
            gv_ref[DW + KS - 1 - j : DW + KS - j, cols] += jnp.sum(sums[j], axis=0, keepdims=True)


def run_bwd(tokens, lengths, saved, gf, gj, wp, pw, kw, vec):
    qkvc, kc, dep, ca, taps, joined, lse = saved
    rows, count = lengths.shape[0], tokens.shape[0]
    length = count // rows

    def body(*refs):
        bwd_kernel(length, *refs)

    full = pl.BlockSpec(memory_space=VM)
    return pl.pallas_call(
        body,
        grid=(rows,),
        out_shape=[
            jax.ShapeDtypeStruct((count, D), bf16),
            jax.ShapeDtypeStruct((D, 4 * ATT), f32),
            jax.ShapeDtypeStruct((D, ATT), f32),
            jax.ShapeDtypeStruct((ATT, LANES), f32),
            jax.ShapeDtypeStruct((VROWS, FF), f32),
        ],
        in_specs=[
            pl.BlockSpec(memory_space=pltpu.SMEM),
            blocked(length, D),
            blocked(length, 4 * ATT),
            blocked(length, ATT),
            blocked(length, D),
            blocked(length, ATT),
            blocked(length, LANES),
            blocked(length, D),
            pl.BlockSpec((1, 8, length), lambda r: (r, 0, 0)),
            blocked(length, D),
            blocked(length, D),
            full,
            full,
            full,
            full,
        ],
        out_specs=[blocked(length, D)] + [full] * 4,
        scratch_shapes=row_scratch(length)
        + [
            VM((3, length + 16, LANES), f32),
            VM((1, length + 16, LANES), f32),
            VM((length, KS * ATT), bf16),
            VM((length, ATT), f32),
            VM((length, 4 * ATT), bf16),
            VM((length, ATT), f32),
        ],
        compiler_params=pltpu.CompilerParams(vmem_limit_bytes=VMEM_LIMIT),
        name="row_backward",
    )(lengths, tokens, qkvc, kc, dep, ca, taps, joined, lse, gf, gj, wp, pw, kw, vec)


def local_layer(tokens, lengths, cotangent, gathered, rows):
    count = gathered.shape[0]
    wp, pw, dw, fi, fo, kw, vec = run_unpack(gathered, rows)
    saved = run_fwd(tokens, lengths, wp, pw, kw, vec)
    output, gf, gj, gdw, gfi, gfo, va = run_mid(tokens, lengths, saved[5], cotangent, dw, fi, fo, vec)
    gt, gp, gpw, gkw, vb = run_bwd(tokens, lengths, saved, gf, gj, wp, pw, kw, vec)
    send = run_pack(count, rows, gp, gpw, gdw, gfi, gfo, gkw, va, vb)
    return output, gt, send


def shards(tokens, doc_lengths, params, cotangent):
    rows = params.shape[0] // LANES
    outer, inner = lax.axis_size("dp"), lax.axis_size("fsdp")
    count = outer * inner
    pad = padded(rows)
    own = jnp.pad(params.reshape(rows, LANES), ((0, pad - rows), (0, 0)))
    gathered = lax.all_gather(own, ("dp", "fsdp"), axis=0, tiled=True).reshape(count, pad, LANES)
    output, gt, send = local_layer(tokens, doc_lengths, cotangent, gathered, rows)
    part = lax.psum_scatter(send.reshape(outer, inner, pad, LANES), "fsdp", scatter_dimension=1, tiled=True)
    part = lax.psum_scatter(part, "dp", scatter_dimension=0, tiled=True).astype(f32)
    part = lax.optimization_barrier(part.reshape(pad, LANES))
    return output, gt, part[:rows].reshape(rows * LANES)


def solution(mesh):
    axes = ("dp", "fsdp")
    placed = (P(axes, None), P(axes, None), P(axes), P(axes, None))
    return jax.shard_map(
        shards,
        mesh=mesh,
        in_specs=placed,
        out_specs=(P(axes, None), P(axes, None), P(axes)),
        check_vma=False,
    )
```

time: 1460 us -> 522 us (0.36); the launches traced: 1430 us -> 517 us
  local copies, waits for them, and re-layouts: 498 us -> 6.66 us
  other arithmetic: 371 us -> 0.99 us
  matrix products: 227 us -> 0 us
  Pallas kernels: 0 us -> 197 us
  waiting for transfers between devices: 321 us -> 299 us
    dot_general x39 -> x0, matrix products: 227 us -> none  [the longest x1 50.9 us: shards(): jnp.einsum('tgi,gio->tgo', normed_low, weights['ffn_in'], preferred_eleme...]
    pallas_call x0 -> x5, Pallas kernels: none -> 197 us  [the longest x1 81.7 us: run_mid(): pl.pallas_call(body, grid=(rows,), out_shape=[jax.ShapeDtypeStruct((count...]
    all_gather x1 -> x0, other arithmetic: 188 us -> none  [shards(): gathered = lax.all_gather(params, ('dp', 'fsdp'), axis=0, tiled=True)]
    concatenate x1 -> x0, local copies, waits for them, and re-layouts: 128 us -> none  [shards(): jnp.concatenate(pieces + [jnp.zeros((gathered.shape[0] - used_size,), f32)])]
    mul x36 -> x0, local copies, waits for them, and re-layouts: 115 us -> none  [the longest x28 93.2 us: shards(): tap_weights[..., tap_index:tap_index + 1]]
    reduce_sum x20 -> x0, other arithmetic: 82.6 us -> none  [the longest x1 34.5 us: shards(): jnp.sum(grad_conv_out * (shift_rows(conv32, tap_index - half_taps) * tap_...]
    reshape x23 -> x1, local copies, waits for them, and re-layouts: 76.2 us -> 0.84 us  [shards(): return (output, gt, part[:rows].reshape(rows * LANES))]
    unnamed x323 -> x4, local copies, waits for them, and re-layouts: 60.5 us -> 4.13 us
  transfers between devices with their start and end apart: 3 -> 3, of which waited for: 3 -> 3; matrix products, arithmetic and copies ran while one was open for 4% -> 0% of each run, Pallas kernels for 0% -> 0%
where the time goes in v1:
time: 522 us; the launch traced here: 517 us
  waiting for transfers between devices  299 us (57%)
  Pallas kernels  197 us (38%)
  between operations  14 us (3%)
  local copies, waits for them, and re-layouts  6.66 us (1%)
    unnamed x5, waiting for transfers between devices  214 us
    all_gather x1, waiting for transfers between devices, shards(): lax.all_gather(own, ('dp', 'fsdp'), axis=0, tiled=True)  84.3 us
    pallas_call x1, Pallas kernels, run_mid(): pl.pallas_call(body, grid=(rows,), out_shape=[jax.ShapeDtypeStruct((count...  81.7 us
    pallas_call x1, Pallas kernels, run_bwd(): pl.pallas_call(body, grid=(rows,), out_shape=[jax.ShapeDtypeStruct((count...  62.6 us
    pallas_call x1, Pallas kernels, run_fwd(): pl.pallas_call(body, grid=(rows,), out_shape=[jax.ShapeDtypeStruct((count...  30.9 us
    pallas_call x1, Pallas kernels, run_pack(): pl.pallas_call(body, out_shape=jax.ShapeDtypeStruct((count, padded(rows),...  12.2 us
  transfers between devices with their start and end apart: 3, of which 3 were waited for; matrix products, arithmetic and copies ran while one was open for 0% of the time, Pallas kernels for 0%

profile of v1, /device:TPU:2, one launch (start us, length us, event | category | flops | bytes accessed | tf_op | source)
XLA Modules:
  0.0 517.1 jit_solution(1547083124289681488)
XLA Ops:
  7.2 0.0 all-gather.2.cloned.1.call-start
  7.2 1.7 pad.4
  8.9 0.0 all-gather.2.cloned.1.call-update
  8.9 0.0 all-reduce.5.cloned.1.call-start
  9.0 84.3 %all-gather.2.cloned.1.call-done = bf16[35328,128]{1,0:T(8,128)(2,1)} async-done(((bf16[1104,128]{1,0:T(8,128)(2,1)}), bf16[35328,128]{1,0:T(8,128)(2,1)}) %all-gather.2.cloned.1.call-update) | async-done | bytes 9043984 | tf_op jit(solution)/shard_map/all_gather | solution.py:794
  93.3 9.2 %unpack.1 = (bf16[768,1536]{1,0:T(8,128)(2,1)}, bf16[768,384]{1,0:T(8,128)(2,1)}, bf16[768,768]{1,0:T(8,128)(2,1)}, bf16[768,1536]{1,0:T(8,128)(2,1)}, bf16[3072...) custom-call(bf16[32,1104,128]{2,1,0:T(8,128)(2,1)} %bitcast.17), custom_call_target="tpu_custom_call" | custom-call | tf_op jit(solution)/shard_map/unpack/pallas_call | solution.py:171
  102.5 30.9 %row_forward.1 = (bf16[1536,1536]{1,0:T(8,128)(2,1)}, bf16[1536,384]{1,0:T(8,128)(2,1)}, bf16[1536,768]{1,0:T(8,128)(2,1)}, bf16[1536,384]{1,0:T(8,128)(2,1)}, f...) custom-call(s32[3,16]{1,0:T(4,128)} %refs_0_.5, bf16[1536,768]{1,0:T(8,128)(2,1)} %refs_1_.5, ...), custom_call_target="tpu_custom_call" | custom-call | tf_op jit(solution)/shard_map/row_forward/pallas_call | solution.py:417
  133.4 81.7 %mid.1 = (bf16[1536,768]{1,0:T(8,128)(2,1)}, bf16[1536,768]{1,0:T(8,128)(2,1)}, bf16[1536,768]{1,0:T(8,128)(2,1)}, f32[768,768]{1,0:T(8,128)}, f32[768,1536]{1,0...) custom-call(s32[3,16]{1,0:T(4,128)} %refs_0_.5, bf16[1536,768]{1,0:T(8,128)(2,1)} %refs_1_.5, ...), custom_call_target="tpu_custom_call" | custom-call | tf_op jit(solution)/shard_map/mid/pallas_call | solution.py:575
  215.1 62.6 %row_backward.1 = (bf16[1536,768]{1,0:T(8,128)(2,1)}, f32[768,1536]{1,0:T(8,128)}, f32[768,384]{1,0:T(8,128)}, f32[384,128]{1,0:T(8,128)}, f32[24,3072]{1,0:T(8,128)}) custom-call(s32[3,16]{1,0:T(4,128)} %refs_0_.5, bf16[1536,768]{1,0:T(8,128)(2,1)} %refs_1_.5, bf16[1536,1536]{1,0:T(8,128)(2,1)} %get-tuple-element.38.refs_2_, ...), custom_call_target="tpu_custom_call" | custom-call | tf_op jit(solution)/shard_map/row_backward/pallas_call | solution.py:736
  277.7 12.2 %pack.1 = bf16[32,1104,128]{2,1,0:T(8,128)(2,1)} custom-call(f32[768,1536]{1,0:T(8,128)} %get-tuple-element.47.refs_0_, f32[768,384]{1,0:T(8,128)} %get-tuple-element.48.refs_1_, f32[768,768]{1,0:T(8,128)} %get-tuple-element.49.refs_2_, f32[768,1536]{1,0:T(8,128)} %get-tuple-element.50.refs_3_, f32[3072,384]{1,0:T(8,128)} %get-tuple-element.51.refs_4_, ...), custom_call_target="tpu_custom_call" | custom-call | tf_op jit(solution)/shard_map/pack/pallas_call | solution.py:251
  289.9 0.0 copy-start
  289.9 0.0 all-reduce.5.cloned.1.call-update
  289.9 0.0 reduce-scatter.7.cloned.1.call-start
  290.0 0.6 copy-done
  290.5 0.6 dynamic-slice
  291.1 185.5 %all-reduce.5.cloned.1.call-done = bf16[4,8,1104,128]{3,2,1,0:T(8,128)(2,1)} async-done(((bf16[4,8,1104,128]{3,2,1,0:T(8,128)(2,1)}), bf16[4,8,1104,128]{3,2,1,0:T(8,128)(2,1)}) %all-reduce.5.cloned.1.call-update) | async-done | bytes 9043984
  476.7 3.0 constant_dynamic-slice_fusion
  479.6 0.0 reduce-scatter.7.cloned.1.call-update
  479.7 28.9 %reduce-scatter.7.cloned.1.call-done = bf16[1,1,1104,128]{3,2,1,0:T(8,128)(2,1)} async-done(((bf16[4,1,1104,128]{3,2,1,0:T(8,128)(2,1)}), bf16[1,1,1104,128]{3,2,1,0:T(8,128)(2,1)}) %reduce-scatter.7.cloned.1.call-update) | async-done | bytes 282640
  508.5 1.0 bitcast_convert_fusion
  509.5 0.8 slice_bitcast_fusion
Async XLA Ops:
  7.2 86.1 %all-gather.2.cloned.1.call-start = ((), (), s32[]{:S(2)}) async-start(), calls=%async_computation.1 | async-start | bytes 9326592 | tf_op jit(solution)/shard_map/all_gather | solution.py:794
  8.9 467.7 %all-reduce.5.cloned.1.call-start = ((), (), s32[]{:S(2)}) async-start(), calls=%async_computation.2 | async-start | bytes 18087936
  289.9 0.7 copy-start
  289.9 218.6 %reduce-scatter.7.cloned.1.call-start = ((), (), s32[]{:S(2)}) async-start(), calls=%async_computation.3 | async-start | bytes 1413120
Sparse Core Ops, SparseCore 0:
  11.6 81.6 all-gather.1
  290.0 186.5 all-reduce.4
  479.9 28.5 reduce-scatter.6

commit v2 on v1

--- a/solution.py
+++ b/solution.py
@@ -775,6 +775,237 @@
     )(lengths, tokens, qkvc, kc, dep, ca, taps, joined, lse, gf, gj, wp, pw, kw, vec)
 
 
+class Place:
+    def __init__(self, outer, inner):
+        self.outer, self.inner = outer, inner
+        self.lines = inner // 2
+        dp, fs = lax.axis_index("dp"), lax.axis_index("fsdp")
+        self.y, self.x, self.z, self.c = dp // 2, lax.rem(dp, 2), fs // 2, lax.rem(fs, 2)
+
+    def coords(self, dy=0, dx=0, dz=0, dc=0):
+        def other(v, d):
+            if d == 0:
+                return v
+            out, bit = 0, 1
+            while bit <= max(d, self.lines - 1, 1):
+                digit = lax.rem(v // bit, 2)
+                out = out + bit * ((1 - digit) if d & bit else digit)
+                bit *= 2
+            return out
+
+        return other(self.y, dy) * 2 + other(self.x, dx), other(self.z, dz) * 2 + other(self.c, dc)
+
+    def index(self, **d):
+        o, i = self.coords(**d)
+        return o * self.inner + i
+
+
+def greet(peers):
+    barrier = pltpu.get_barrier_semaphore()
+    for peer in peers:
+        pl.semaphore_signal(barrier, inc=1, device_id=peer, device_id_type=pl.DeviceIdType.MESH)
+    pl.semaphore_wait(barrier, len(peers))
+
+
+def peers_of(place):
+    return [place.coords(dz=d) for d in range(1, place.lines)] + [
+        place.coords(dx=1),
+        place.coords(dy=1),
+        place.coords(dc=1),
+    ]
+
+
+class Copies:
+    def __init__(self, send, recv):
+        self.send, self.recv, self.used, self.made = send, recv, 0, []
+
+    def start(self, src, dst, peer, slot):
+        copy = pltpu.make_async_remote_copy(
+            src_ref=src,
+            dst_ref=dst,
+            send_sem=self.send.at[self.used],
+            recv_sem=self.recv.at[slot],
+            device_id=peer,
+            device_id_type=pl.DeviceIdType.MESH,
+        )
+        self.used += 1
+        copy.start()
+        self.made.append(copy)
+
+    def arrived(self, dst, slot):
+        pltpu.make_async_copy(dst, dst, self.recv.at[slot]).wait()
+
+    def finish(self):
+        for copy in self.made:
+            copy.wait_send()
+
+
+def gather_kernel(outer, inner, pad, own_ref, out_ref, send, recv):
+    place = Place(outer, inner)
+    lines = place.lines
+    cut = -(-pad // 32) * 16
+    parts = {"a": pl.ds(0, cut), "b": pl.ds(cut, pad - cut)}
+    me = place.index()
+    out_ref[me] = own_ref[...]
+    greet(peers_of(place))
+    xp, yp, cp = place.coords(dx=1), place.coords(dy=1), place.coords(dc=1)
+    copies = Copies(send, recv)
+    Z, X, Y, A, B, OTHER = (lines * k for k in range(6))
+
+    def whole(at):
+        return out_ref.at[at]
+
+    def half(at, which):
+        return out_ref.at[at, parts[which]]
+
+    def on(ref, peer, slot):
+        copies.start(ref, ref, peer, slot)
+
+    for d in range(1, lines):
+        on(whole(me), place.coords(dz=d), Z + d)
+    on(whole(me), xp, X)
+    on(whole(me), yp, Y)
+    on(whole(me), cp, OTHER + Z)
+    for d in range(1, lines):
+        at = place.index(dz=d)
+        copies.arrived(whole(at), Z + d)
+        on(whole(at), xp, X + d)
+        on(whole(at), yp, Y + d)
+        on(whole(at), cp, OTHER + Z + d)
+    for d in range(lines):
+        at = place.index(dz=d, dx=1)
+        copies.arrived(whole(at), X + d)
+        on(half(at, "a"), yp, A + d)
+        on(whole(at), cp, OTHER + X + d)
+        at = place.index(dz=d, dy=1)
+        copies.arrived(whole(at), Y + d)
+        on(half(at, "b"), xp, B + d)
+        on(whole(at), cp, OTHER + Y + d)
+    for d in range(lines):
+        at = place.index(dz=d, dy=1, dx=1)
+        copies.arrived(half(at, "a"), A + d)
+        on(half(at, "a"), cp, OTHER + A + d)
+        copies.arrived(half(at, "b"), B + d)
+        on(half(at, "b"), cp, OTHER + B + d)
+    for d in range(lines):
+        copies.arrived(whole(place.index(dz=d, dc=1)), OTHER + Z + d)
+        copies.arrived(whole(place.index(dz=d, dx=1, dc=1)), OTHER + X + d)
+        copies.arrived(whole(place.index(dz=d, dy=1, dc=1)), OTHER + Y + d)
+        at = place.index(dz=d, dy=1, dx=1, dc=1)
+        copies.arrived(half(at, "a"), OTHER + A + d)
+        copies.arrived(half(at, "b"), OTHER + B + d)
+    copies.finish()
+
+
+def run_gather(own, outer, inner):
+    pad = own.shape[0]
+    lines = inner // 2
+
+    def body(*refs):
+        gather_kernel(outer, inner, pad, *refs)
+
+    return pl.pallas_call(
+        body,
+        out_shape=jax.ShapeDtypeStruct((outer * inner, pad, LANES), bf16),
+        in_specs=[pl.BlockSpec(memory_space=VM)],
+        out_specs=pl.BlockSpec(memory_space=VM),
+        scratch_shapes=[pltpu.SemaphoreType.DMA((11 * lines,)), pltpu.SemaphoreType.DMA((10 * lines,))],
+        compiler_params=pltpu.CompilerParams(
+            vmem_limit_bytes=VMEM_LIMIT, collective_id=0, has_side_effects=True
+        ),
+        name="gather",
+    )(own)
+
+
+def scatter_kernel(outer, inner, rows, pad, part_ref, out_ref, work, rc, ry, rx, ry2, rx2, rz, send, recv):
+    place = Place(outer, inner)
+    lines = place.lines
+    cut = -(-pad // 32) * 16
+    a, b = pl.ds(0, cut), pl.ds(cut, pad - cut)
+    every = pl.ds(0, pad)
+    greet(peers_of(place))
+    xp, yp, cp = place.coords(dx=1), place.coords(dy=1), place.coords(dc=1)
+    copies = Copies(send, recv)
+    C, YA, XB, XA, YB, Z = (lines * k for k in (0, 4, 6, 8, 9, 10))
+
+    def at(dy, dx, d):
+        return (dy * 2 + dx) * lines + d
+
+    order = [(dy, dx, d) for dy, dx in ((1, 1), (1, 0), (0, 1), (0, 0)) for d in range(lines)]
+    for dy, dx, d in order:
+        k = at(dy, dx, d)
+        copies.start(part_ref.at[place.index(dy=dy, dx=dx, dz=d, dc=1)], rc.at[k], cp, C + k)
+
+    def plus(k, rows_, other):
+        work[k, rows_] = (work[k, rows_].astype(f32) + other.astype(f32)).astype(bf16)
+
+    for dy, dx, d in order:
+        k = at(dy, dx, d)
+        copies.arrived(rc.at[k], C + k)
+        work[k] = (part_ref[place.index(dy=dy, dx=dx, dz=d)].astype(f32) + rc[k].astype(f32)).astype(bf16)
+        if dy:
+            copies.start(work.at[k, a], ry.at[dx * lines + d], yp, YA + dx * lines + d)
+        if dx:
+            copies.start(work.at[k, b], rx.at[dy * lines + d], xp, XB + dy * lines + d)
+    for d in range(lines):
+        n = lines + d
+        copies.arrived(ry.at[n], YA + n)
+        plus(at(0, 1, d), a, ry[n])
+        copies.start(work.at[at(0, 1, d), a], rx2.at[d], xp, XA + d)
+        copies.arrived(rx.at[n], XB + n)
+        plus(at(1, 0, d), b, rx[n])
+        copies.start(work.at[at(1, 0, d), b], ry2.at[d], yp, YB + d)
+    for d in reversed(range(lines)):
+        k = at(0, 0, d)
+        copies.arrived(ry.at[d], YA + d)
+        copies.arrived(rx.at[d], XB + d)
+        copies.arrived(rx2.at[d], XA + d)
+        copies.arrived(ry2.at[d], YB + d)
+        top = work[k, a].astype(f32) + ry[d].astype(f32) + rx2[d].astype(f32)
+        low = work[k, b].astype(f32) + rx[d].astype(f32) + ry2[d].astype(f32)
+        work[k, a] = top.astype(bf16)
+        work[k, b] = low.astype(bf16)
+        if d:
+            copies.start(work.at[k], rz.at[d], place.coords(dz=d), Z + d)
+    total = work[at(0, 0, 0)].astype(f32)
+    for d in range(1, lines):
+        copies.arrived(rz.at[d], Z + d)
+        total = total + rz[d].astype(f32)
+    out_ref[...] = total[0:rows]
+    copies.finish()
+
+
+def run_scatter(part, rows, outer, inner):
+    pad = part.shape[1]
+    lines = inner // 2
+    cut = -(-pad // 32) * 16
+
+    def body(*refs):
+        scatter_kernel(outer, inner, rows, pad, *refs)
+
+    return pl.pallas_call(
+        body,
+        out_shape=jax.ShapeDtypeStruct((rows, LANES), f32),
+        in_specs=[pl.BlockSpec(memory_space=VM)],
+        out_specs=pl.BlockSpec(memory_space=VM),
+        scratch_shapes=[
+            VM((4 * lines, pad, LANES), bf16),
+            VM((4 * lines, pad, LANES), bf16),
+            VM((2 * lines, cut, LANES), bf16),
+            VM((2 * lines, pad - cut, LANES), bf16),
+            VM((lines, pad - cut, LANES), bf16),
+            VM((lines, cut, LANES), bf16),
+            VM((lines, pad, LANES), bf16),
+            pltpu.SemaphoreType.DMA((11 * lines,)),
+            pltpu.SemaphoreType.DMA((11 * lines,)),
+        ],
+        compiler_params=pltpu.CompilerParams(
+            vmem_limit_bytes=VMEM_LIMIT, collective_id=1, has_side_effects=True
+        ),
+        name="scatter",
+    )(part)
+
+
 def local_layer(tokens, lengths, cotangent, gathered, rows):
     count = gathered.shape[0]
     wp, pw, dw, fi, fo, kw, vec = run_unpack(gathered, rows)
@@ -788,15 +1019,11 @@
 def shards(tokens, doc_lengths, params, cotangent):
     rows = params.shape[0] // LANES
     outer, inner = lax.axis_size("dp"), lax.axis_size("fsdp")
-    count = outer * inner
-    pad = padded(rows)
-    own = jnp.pad(params.reshape(rows, LANES), ((0, pad - rows), (0, 0)))
-    gathered = lax.all_gather(own, ("dp", "fsdp"), axis=0, tiled=True).reshape(count, pad, LANES)
+    own = jnp.pad(params.reshape(rows, LANES), ((0, padded(rows) - rows), (0, 0)))
+    gathered = run_gather(own, outer, inner)
     output, gt, send = local_layer(tokens, doc_lengths, cotangent, gathered, rows)
-    part = lax.psum_scatter(send.reshape(outer, inner, pad, LANES), "fsdp", scatter_dimension=1, tiled=True)
-    part = lax.psum_scatter(part, "dp", scatter_dimension=0, tiled=True).astype(f32)
-    part = lax.optimization_barrier(part.reshape(pad, LANES))
-    return output, gt, part[:rows].reshape(rows * LANES)
+    part = run_scatter(send, rows, outer, inner)
+    return output, gt, part.reshape(rows * LANES)
 
 
 def solution(mesh):

time: 522 us -> 325 us (0.62)
  waiting for transfers between devices: 299 us -> 0 us
  Pallas kernels: 197 us -> 315 us
  between operations: 14 us -> 0.85 us
    unnamed x5 -> x0, waiting for transfers between devices: 214 us -> none
    pallas_call x0 -> x2, Pallas kernels: none -> 129 us  [the longest x1 73.1 us: run_scatter(): pl.pallas_call(body, out_shape=jax.ShapeDtypeStruct((rows, LANES), f32),...]
    all_gather x1 -> x0, waiting for transfers between devices: 84.3 us -> none  [shards(): lax.all_gather(own, ('dp', 'fsdp'), axis=0, tiled=True)]
    pallas_call x1, Pallas kernels: 62.6 us -> 52.4 us  [run_bwd(): pl.pallas_call(body, grid=(rows,), out_shape=[jax.ShapeDtypeStruct((count...]
  transfers between devices with their start and end apart: 3 -> 0, of which waited for: 3 -> 0; matrix products, arithmetic and copies ran while one was open for 0% -> 0% of each run, Pallas kernels for 0% -> 0%
where the time goes in v2:
time: 325 us; the launch traced here: 320 us
  Pallas kernels  315 us (97%)
  local copies, waits for them, and re-layouts  3.59 us (1%)
    pallas_call x1, Pallas kernels, run_mid(): pl.pallas_call(body, grid=(rows,), out_shape=[jax.ShapeDtypeStruct((count...  81.7 us
    pallas_call x1, Pallas kernels, run_scatter(): pl.pallas_call(body, out_shape=jax.ShapeDtypeStruct((rows, LANES), f32),...  73.1 us
    pallas_call x1, Pallas kernels, run_gather(): pl.pallas_call(body, out_shape=jax.ShapeDtypeStruct((outer * inner, pad,...  55.6 us
    pallas_call x1, Pallas kernels, run_bwd(): pl.pallas_call(body, grid=(rows,), out_shape=[jax.ShapeDtypeStruct((count...  52.4 us
    pallas_call x1, Pallas kernels, run_fwd(): pl.pallas_call(body, grid=(rows,), out_shape=[jax.ShapeDtypeStruct((count...  31.1 us
    pallas_call x1, Pallas kernels, run_pack(): pl.pallas_call(body, out_shape=jax.ShapeDtypeStruct((count, padded(rows),...  12.2 us
    pallas_call x1, Pallas kernels, run_unpack(): pl.pallas_call(body, out_shape=out, in_specs=[pl.BlockSpec(memory_space=V...  9.17 us

profile of v2, /device:TPU:2, one launch (start us, length us, event | category | flops | bytes accessed | tf_op | source)
XLA Modules:
  0.0 319.7 jit_solution(6042466258102205411)
XLA Ops:
  0.6 1.7 pad.4.refs_0_
  2.3 55.6 %gather.1.refs_0_ = bf16[32,1104,128]{2,1,0:T(8,128)(2,1)} custom-call(bf16[1104,128]{1,0:T(8,128)(2,1)} %pad.4.refs_0_), custom_call_target="tpu_custom_call" | custom-call | tf_op jit(solution)/shard_map/gather/pallas_call | solution.py:907
  57.9 9.2 %unpack.1 = (bf16[768,1536]{1,0:T(8,128)(2,1)}, bf16[768,384]{1,0:T(8,128)(2,1)}, bf16[768,768]{1,0:T(8,128)(2,1)}, bf16[768,1536]{1,0:T(8,128)(2,1)}, bf16[3072...) custom-call(bf16[32,1104,128]{2,1,0:T(8,128)(2,1)} %gather.1.refs_0_), custom_call_target="tpu_custom_call" | custom-call | tf_op jit(solution)/shard_map/unpack/pallas_call | solution.py:171
  67.1 31.1 %row_forward.1 = (bf16[1536,1536]{1,0:T(8,128)(2,1)}, bf16[1536,384]{1,0:T(8,128)(2,1)}, bf16[1536,768]{1,0:T(8,128)(2,1)}, bf16[1536,384]{1,0:T(8,128)(2,1)}, f...) custom-call(s32[3,16]{1,0:T(4,128)} %refs_0_.5, bf16[1536,768]{1,0:T(8,128)(2,1)} %refs_1_.5, ...), custom_call_target="tpu_custom_call" | custom-call | tf_op jit(solution)/shard_map/row_forward/pallas_call | solution.py:417
  98.2 81.7 %mid.1 = (bf16[1536,768]{1,0:T(8,128)(2,1)}, bf16[1536,768]{1,0:T(8,128)(2,1)}, bf16[1536,768]{1,0:T(8,128)(2,1)}, f32[768,768]{1,0:T(8,128)}, f32[768,1536]{1,0...) custom-call(s32[3,16]{1,0:T(4,128)} %refs_0_.5, bf16[1536,768]{1,0:T(8,128)(2,1)} %refs_1_.5, ...), custom_call_target="tpu_custom_call" | custom-call | tf_op jit(solution)/shard_map/mid/pallas_call | solution.py:575
  179.9 52.4 %row_backward.1 = (bf16[1536,768]{1,0:T(8,128)(2,1)}, f32[768,1536]{1,0:T(8,128)}, f32[768,384]{1,0:T(8,128)}, f32[384,128]{1,0:T(8,128)}, f32[24,3072]{1,0:T(8,128)}) custom-call(s32[3,16]{1,0:T(4,128)} %refs_0_.5, bf16[1536,768]{1,0:T(8,128)(2,1)} %refs_1_.5, bf16[1536,1536]{1,0:T(8,128)(2,1)} %get-tuple-element.38.refs_2_, ...), custom_call_target="tpu_custom_call" | custom-call | tf_op jit(solution)/shard_map/row_backward/pallas_call | solution.py:736
  232.3 12.2 %pack.1.refs_0_ = bf16[32,1104,128]{2,1,0:T(8,128)(2,1)} custom-call(f32[768,1536]{1,0:T(8,128)} %get-tuple-element.47.refs_0_, f32[768,384]{1,0:T(8,128)} %get-tuple-element.48.refs_1_, f32[768,768]{1,0:T(8,128)} %get-tuple-element.49.refs_2_, f32[768,1536]{1,0:T(8,128)} %get-tuple-element.50.refs_3_, f32[3072,384]{1,0:T(8,128)} %get-tuple-element.51.refs_4_, ...), custom_call_target="tpu_custom_call" | custom-call | tf_op jit(solution)/shard_map/pack/pallas_call | solution.py:251
  244.5 73.1 %scatter.1 = f32[1090,128]{1,0:T(8,128)} custom-call(bf16[32,1104,128]{2,1,0:T(8,128)(2,1)} %pack.1.refs_0_), custom_call_target="tpu_custom_call" | custom-call | tf_op jit(solution)/shard_map/scatter/pallas_call | solution.py:986
  317.6 1.9 copy.8

commit v3 on v1

--- a/solution.py
+++ b/solution.py
@@ -26,23 +26,13 @@
 bf16 = jnp.bfloat16
 i32 = jnp.int32
 
-PIECES = [
-    ("proj", 4 * D, ATT),
-    ("point", D, ATT),
-    ("dense", D, D),
-    ("ffn_in", D, FF // GROUPS),
-    ("ffn_out", FF, D // GROUPS),
-]
-START = {}
-_at = 0
-for _name, _r, _c in PIECES:
-    START[_name] = _at
-    _at += _r * _c // LANES
-START["depth"] = _at
-START["kernel"] = _at + KS * D // LANES
-START["bias4"] = START["kernel"] + ATT * HEADS * KS // LANES
-START["tail"] = START["bias4"] + 4 * ATT // LANES
-USED = START["tail"] + 61
+FIRST = 5 * D * ATT // LANES
+MATRICES = FIRST + (D * D + 2 * D * FF // GROUPS) // LANES
+DEPTH_AT = 0
+KERNEL_AT = KS * D // LANES
+BIAS_AT = KERNEL_AT + ATT * HEADS * KS // LANES
+TAIL_AT = BIAS_AT + 4 * ATT // LANES
+SMALL = TAIL_AT + 61
 KB = HEADS * KS
 
 QB, VB, CB, PB, KBR, DB, N1G, N1S, FIB, FOB, N2G, N2S, DW = range(13)
@@ -92,42 +82,104 @@
     return -(-rows // 16) * 16
 
 
-def unpack_kernel(count, rows, g_ref, wp_ref, pw_ref, dw_ref, fi_ref, fo_ref, kw_ref, vec_ref, flat, kwt):
-    pad = padded(rows)
-
-    def spread(i):
-        flat[pl.ds(i * rows, pad), :] = g_ref[i].astype(f32)
-
-    for i in range(count):
-        spread(i)
-
-    def piece(name, out, height, width, row0, col0, skip):
+class Section:
+    def __init__(self, base, kinds, chunk, small, rows, count, inner):
+        self.base, self.chunk, self.rows, self.count, self.inner = base, chunk, rows, count, inner
+        self.main = sum(n for n, _ in kinds)
+        self.small = -(-SMALL // chunk) if small else 0
+        self.kinds = kinds + ([(self.small, 1)] if small else [])
+        self.used = self.main + self.small
+        self.pieces = -(-rows // chunk) + 1
+        self.slots = self.pieces + self.small
+        self.sources = (chunk - 2) // rows + 2
+
+    def start(self, v):
+        at = self.base + v * self.chunk
+        if self.small:
+            at = jnp.where(v >= self.main, MATRICES + (v - self.main) * self.chunk, at)
+        return at
+
+    def first_piece(self, i):
+        return jnp.maximum(self.rows * i - self.base, 0) // self.chunk
+
+    def of_owner(self, i, k):
+        if k < self.pieces:
+            v = self.first_piece(i) + k
+            ok = v < self.main
+        else:
+            v = self.main + k - self.pieces + 0 * i
+            ok = v >= 0
+        at = self.start(v)
+        return v, ok & (at < self.rows * (i + 1)) & (at + self.chunk > self.rows * i)
+
+    def of_chunk(self, v, s):
+        i = self.start(v) // self.rows + s
+        return i, (v < self.used) & (i < self.count) & (self.rows * i < self.start(v) + self.chunk)
+
+    def source_of(self, v, i):
+        return i - self.start(v) // self.rows
+
+    def slot_of(self, v, i):
+        return jnp.where(v < self.main, v - self.first_piece(i), self.pieces + v - self.main)
+
+    def by_kind(self, v, action):
+        at, seen = 0, {}
+        for n, per in self.kinds:
+            seen.setdefault(per, []).append((at, at + n))
+            at += n
+        for per, spans in seen.items():
+            ok = False
+            for lo, hi in spans:
+                ok = ((v >= lo) & (v < hi)) | ok
+            pl.when(ok)(lambda per=per: action(per))
+
+
+def sections(count, rows, inner):
+    big, little = 24576 // count, 12288 // count
+    first = Section(0, [(FIRST // little, 3)], little, True, rows, count, inner)
+    kinds = [(D * n // LANES // big, n // LANES) for n in (D, FF // GROUPS)] + [(FF * 3 // big, 3)]
+    return first, Section(FIRST, kinds, big, False, rows, count, inner)
+
+
+def to_frames(part, pieces):
+    chunk, v = part.shape[1], 0
+    for ref, height, width, col in pieces:
         per = width // LANES
-        base = START[name] + skip
-        for c in range(per):
-            for r in range(0, height, 256):
-                part = min(256, height - r)
-                out[row0 + r : row0 + r + part, col0 + c * LANES : col0 + (c + 1) * LANES] = flat[
-                    pl.ds(base + r * per + c, part, stride=per), :
+        tall = chunk // per
+        for r in range(0, height, tall):
+            for c in range(per):
+                part[v, c * tall : (c + 1) * tall, :] = ref[
+                    r : r + tall, col + c * LANES : col + (c + 1) * LANES
                 ].astype(bf16)
-
-    for m in range(4):
-        piece("proj", wp_ref, D, ATT, 0, m * ATT, m * D * ATT // LANES)
-    piece("point", pw_ref, D, ATT, 0, 0, 0)
-    piece("dense", dw_ref, D, D, 0, 0, 0)
-    piece("ffn_in", fi_ref, D, FF // GROUPS, 0, 0, 0)
-    piece("ffn_out", fo_ref, FF, D // GROUPS, 0, 0, 0)
-
+            v += 1
+    if v < part.shape[0]:
+        part[v:] = jnp.zeros((part.shape[0] - v, chunk, LANES), bf16)
+    return v
+
+
+def from_frames(buf, pieces):
+    chunk, v = buf.shape[1], 0
+    for ref, height, width, col in pieces:
+        per = width // LANES
+        tall = chunk // per
+        for r in range(0, height, tall):
+            for c in range(per):
+                ref[r : r + tall, col + c * LANES : col + (c + 1) * LANES] = buf[v, c * tall : (c + 1) * tall, :]
+            v += 1
+    return v
+
+
+def unpack_small(flat, kw_ref, vec_ref, kwt):
     vec_ref[...] = jnp.zeros_like(vec_ref)
     for row in range(4):
         for c in range(3):
-            at = START["bias4"] + row * 3 + c
+            at = BIAS_AT + row * 3 + c
             vec_ref[row : row + 1, c * LANES : (c + 1) * LANES] = flat[at : at + 1, :]
     for j in range(KS):
         for c in range(6):
-            at = START["depth"] + j * 6 + c
+            at = DEPTH_AT + j * 6 + c
             vec_ref[DW + j : DW + j + 1, c * LANES : (c + 1) * LANES] = flat[at : at + 1, :]
-    at = START["tail"]
+    at = TAIL_AT
     lane = iota((64, LANES), 1)
     first = pltpu.roll(flat[at : at + 64, :], LANES - KB, 1)
     second = pltpu.roll(flat[at + 1 : at + 65, :], LANES - KB, 1)
@@ -139,7 +191,7 @@
         at += many
     perm = tap_perm()
     lane8 = iota((16, LANES), 1)
-    kb = jnp.broadcast_to(flat[START["tail"] : START["tail"] + 1, :], (16, LANES))
+    kb = jnp.broadcast_to(flat[TAIL_AT : TAIL_AT + 1, :], (16, LANES))
     kb = nn(jnp.where(lane8 < KB, kb, 0.0).astype(bf16), perm)
     kb = jnp.where(used_taps((16, LANES)), kb, NEG)
     vec_ref[KBR : KBR + 1, 0:LANES] = kb[0:1]
@@ -147,7 +199,7 @@
     lane = iota((8, LANES), 1)
     for a in range(64):
         c0, ln = divmod(a * KB, LANES)
-        at = START["kernel"] + c0
+        at = KERNEL_AT + c0
         x = pltpu.roll(flat[pl.ds(at, 8, stride=27), :], (LANES - ln) % LANES, 1)
         if ln + KB > LANES:
             y = pltpu.roll(flat[pl.ds(at + 1, 8, stride=27), :], (LANES - ln) % LANES, 1)
@@ -156,59 +208,15 @@
     kw_ref[...] = nn(kwt[0:ATT, :].astype(bf16), perm).astype(bf16)
 
 
-def flat_rows(count, rows):
-    return -(-(max((count - 1) * rows + padded(rows), USED + 240)) // 8) * 8
-
-
-def run_unpack(gathered, rows):
-    count = gathered.shape[0]
-    shapes = [(D, 4 * ATT), (D, ATT), (D, D), (D, FF // GROUPS), (FF, D // GROUPS), (ATT, LANES)]
-    out = [jax.ShapeDtypeStruct(s, bf16) for s in shapes] + [jax.ShapeDtypeStruct((VROWS, FF), f32)]
-
-    def body(*refs):
-        unpack_kernel(count, rows, *refs)
-
-    return pl.pallas_call(
-        body,
-        out_shape=out,
-        in_specs=[pl.BlockSpec(memory_space=VM)],
-        out_specs=[pl.BlockSpec(memory_space=VM)] * len(out),
-        scratch_shapes=[VM((flat_rows(count, rows), LANES), f32), VM((512, LANES), f32)],
-        compiler_params=pltpu.CompilerParams(vmem_limit_bytes=VMEM_LIMIT),
-        name="unpack",
-    )(gathered)
-
-
-def pack_kernel(count, rows, gp_ref, gpw_ref, gdw_ref, gfi_ref, gfo_ref, gkw_ref, va_ref, vb_ref, send_ref, flat, kwt, vec):
-    total = flat.shape[0]
-    used8 = START["depth"] // 8 * 8
-    flat[used8:total, :] = jnp.zeros((total - used8, LANES), f32)
-    vec[...] = va_ref[...] + vb_ref[...]
-
-    def piece(name, src, height, width, row0, col0, skip):
-        per = width // LANES
-        base = START[name] + skip
-        for c in range(per):
-            for r in range(0, height, 256):
-                part = min(256, height - r)
-                flat[pl.ds(base + r * per + c, part, stride=per), :] = src[
-                    row0 + r : row0 + r + part, col0 + c * LANES : col0 + (c + 1) * LANES
-                ]
-
-    for m in range(4):
-        piece("proj", gp_ref, D, ATT, 0, m * ATT, m * D * ATT // LANES)
-    piece("point", gpw_ref, D, ATT, 0, 0, 0)
-    piece("dense", gdw_ref, D, D, 0, 0, 0)
-    piece("ffn_in", gfi_ref, D, FF // GROUPS, 0, 0, 0)
-    piece("ffn_out", gfo_ref, FF, D // GROUPS, 0, 0, 0)
-
+def pack_small(flat, gkw_ref, vec, kwt):
+    flat[...] = jnp.zeros_like(flat)
     perm = tap_perm()
     kwt[...] = jnp.zeros_like(kwt)
     kwt[0:ATT, :] = nt(gkw_ref[...].astype(bf16), perm)
     lane = iota((8, LANES), 1)
     for a in range(64):
         c0, ln = divmod(a * KB, LANES)
-        at = START["kernel"] + c0
+        at = KERNEL_AT + c0
         x = pltpu.roll(kwt[pl.ds(a, 8, stride=64), :], ln, 1)
         if ln + KB > LANES:
             flat[pl.ds(at, 8, stride=27), :] += jnp.where(lane >= ln, x, 0.0)
@@ -217,11 +225,11 @@
             flat[pl.ds(at, 8, stride=27), :] += x
     for row in range(4):
         for c in range(3):
-            at = START["bias4"] + row * 3 + c
+            at = BIAS_AT + row * 3 + c
             flat[at : at + 1, :] = vec[row : row + 1, c * LANES : (c + 1) * LANES]
     for j in range(KS):
         for c in range(6):
-            at = START["depth"] + j * 6 + c
+            at = DEPTH_AT + j * 6 + c
             flat[at : at + 1, :] = vec[DW + j : DW + j + 1, c * LANES : (c + 1) * LANES]
     kwt[...] = jnp.zeros_like(kwt)
     at = 8
@@ -232,35 +240,442 @@
     lane = iota((72, LANES), 1)
     before = pltpu.roll(kwt[7:79, :], KB, 1)
     here = pltpu.roll(kwt[8:80, :], KB, 1)
-    at = START["tail"]
+    at = TAIL_AT
     flat[at : at + 72, :] = jnp.where(lane < KB, before, here)
     kb = jnp.broadcast_to(vec[KBR : KBR + 1, 0:LANES], (16, LANES))
     kb = nt(jnp.where(used_taps((16, LANES)), kb, 0.0).astype(bf16), perm)
     lane = iota((1, LANES), 1)
     flat[at : at + 1, :] = jnp.where(lane < KB, kb[0:1], flat[at : at + 1, :])
 
-    pad = padded(rows)
-    for i in range(count):
-        send_ref[i] = flat[i * rows : i * rows + pad, :].astype(bf16)
-
-
-def run_pack(count, rows, gp, gpw, gdw, gfi, gfo, gkw, va, vb):
-    def body(*refs):
-        pack_kernel(count, rows, *refs)
-
-    return pl.pallas_call(
-        body,
-        out_shape=jax.ShapeDtypeStruct((count, padded(rows), LANES), bf16),
-        in_specs=[pl.BlockSpec(memory_space=VM)] * 8,
-        out_specs=pl.BlockSpec(memory_space=VM),
-        scratch_shapes=[
-            VM((flat_rows(count, rows), LANES), f32),
-            VM((512, LANES), f32),
-            VM((VROWS, FF), f32),
-        ],
-        compiler_params=pltpu.CompilerParams(vmem_limit_bytes=VMEM_LIMIT),
-        name="pack",
-    )(gp, gpw, gdw, gfi, gfo, gkw, va, vb)
+
+class Place:
+    def __init__(self, outer, inner):
+        self.outer, self.inner, self.count = outer, inner, outer * inner
+        self.lines = inner // 2
+        dp, fs = lax.axis_index("dp"), lax.axis_index("fsdp")
+        self.y, self.x, self.z, self.c = dp // 2, lax.rem(dp, 2), fs // 2, lax.rem(fs, 2)
+        self.me = dp * inner + fs
+
+    def coords(self, dy=0, dx=0, z=None, dc=0):
+        def flip(v, d):
+            return 1 - v if d else v
+
+        z = self.z if z is None else z
+        return flip(self.y, dy) * 2 + flip(self.x, dx), z * 2 + flip(self.c, dc)
+
+    def index(self, **d):
+        o, i = self.coords(**d)
+        return o * self.inner + i
+
+    def device(self, n):
+        return n // self.inner, lax.rem(n, self.inner)
+
+    def item(self, t):
+        s = (t + 1) // 2
+        z = self.z - s if t % 2 else self.z + s
+        return z, (z >= 0) & (z < self.lines), s, t % 2 == 1
+
+    def greet_all(self):
+        barrier = pltpu.get_barrier_semaphore()
+        for n in range(1, self.count):
+            peer = self.device(lax.rem(self.me + n, self.count))
+            pl.semaphore_signal(barrier, inc=1, device_id=peer, device_id_type=pl.DeviceIdType.MESH)
+        pl.semaphore_wait(barrier, self.count - 1)
+
+
+class Copies:
+    def __init__(self, send, recv):
+        self.send, self.recv, self.used, self.made = send, recv, 0, []
+
+    def start(self, src, dst, peer, slot, ok=None):
+        number = self.used
+        self.used += 1
+        assert number < self.send.shape[0]
+
+        def make():
+            return pltpu.make_async_remote_copy(
+                src_ref=src(),
+                dst_ref=dst(),
+                send_sem=self.send.at[number],
+                recv_sem=self.recv.at[slot() if callable(slot) else slot],
+                device_id=peer(),
+                device_id_type=pl.DeviceIdType.MESH,
+            )
+
+        self.made.append((make, ok))
+        guarded(ok, lambda: make().start())
+
+    def arrived(self, dst, slot, ok=None):
+        def wait():
+            ref = dst()
+            pltpu.make_async_copy(ref, ref, self.recv.at[slot]).wait()
+
+        guarded(ok, wait)
+
+    def finish(self):
+        for make, ok in self.made:
+            guarded(ok, lambda make=make: make().wait_send())
+
+
+def guarded(ok, action):
+    if ok is None:
+        action()
+    else:
+        pl.when(ok())(action)
+
+
+def half_of(chunk):
+    return -(-chunk // 32) * 16
+
+
+class Gather:
+    @staticmethod
+    def scratch(sect, inner):
+        lines = inner // 2
+        items = 2 * lines - 1
+        return [
+            VM((sect.count, sect.chunk, LANES), bf16),
+            VM((sect.rows + 2 * sect.chunk + 16, LANES), f32),
+            VM((sect.slots, sect.chunk, LANES), bf16),
+            VM((sect.sources, sect.chunk, LANES), bf16),
+            VM((sect.chunk, LANES), f32),
+            pltpu.SemaphoreType.DMA((sect.slots + 10 * items + 4,)),
+            pltpu.SemaphoreType.DMA((sect.sources + 9 * items,)),
+        ]
+
+    def __init__(self, sect, place, own_ref, scratch):
+        self.sect, self.place, self.own = sect, place, own_ref
+        self.buf, self.ownf, self.win, self.land, self.frame, send, recv = scratch
+        self.copies = Copies(send, recv)
+        n = 2 * place.lines - 1
+        self.items = n
+        self.Z, self.X, self.Y, self.A, self.B, self.CZ, self.CX, self.CY, self.CD = (sect.sources + n * k for k in range(9))
+        cut = half_of(sect.chunk)
+        self.half = {"a": pl.ds(0, cut), "b": pl.ds(cut, sect.chunk - cut)}
+        self.steps = [self.offer, self.form]
+        for s in range(1, place.lines):
+            self.steps.append(lambda s=s: self.along(s))
+            self.steps.append(lambda s=s: self.across(s - 1))
+        self.steps.append(lambda: self.across(place.lines - 1))
+        self.steps.append(self.diagonal)
+        self.steps.append(self.rest)
+
+    def greet(self):
+        self.place.greet_all()
+
+    def offer(self):
+        sect, me = self.sect, self.place.me
+        self.ownf[...] = jnp.zeros_like(self.ownf)
+        self.ownf[sect.chunk : sect.chunk + sect.rows, :] = self.own[...].astype(f32)
+        for k in range(sect.slots):
+            self.give(k)
+
+    def give(self, k):
+        sect, place, me = self.sect, self.place, self.place.me
+        v, ok = sect.of_owner(me, k)
+
+        @pl.when(ok)
+        def _():
+            at = sect.chunk + sect.start(v) - sect.rows * me
+            self.win[k] = self.ownf[pl.ds(at, sect.chunk), :].astype(bf16)
+
+        @pl.when(ok & (v == me))
+        def _():
+            self.land[sect.source_of(v, me)] = self.win[k]
+
+        def chunk():
+            return sect.of_owner(me, k)[0]
+
+        def away():
+            v, ok = sect.of_owner(me, k)
+            return ok & (v != me)
+
+        self.copies.start(
+            lambda: self.win.at[k],
+            lambda: self.land.at[sect.source_of(chunk(), me)],
+            lambda: place.device(chunk()),
+            lambda: sect.source_of(chunk(), me),
+            away,
+        )
+
+    def form(self):
+        sect, me = self.sect, self.place.me
+        row = iota((sect.chunk, LANES), 0) + sect.start(me)
+        x = None
+        for s in range(sect.sources):
+            i, ok = sect.of_chunk(me, s)
+            self.copies.arrived(lambda: self.land.at[s], s, lambda: ok & (i != me))
+            here = self.land[s].astype(f32)
+            x = here if x is None else jnp.where(row >= sect.rows * i, here, x)
+        self.frame[...] = x
+
+        def settle(per):
+            tall = sect.chunk // per
+            for c in range(per):
+                self.buf[me, c * tall : (c + 1) * tall, :] = self.frame[pl.ds(c, tall, stride=per), :].astype(bf16)
+
+        sect.by_kind(me, settle)
+
+        @pl.when(me >= sect.used)
+        def _():
+            self.buf[me] = jnp.zeros((sect.chunk, LANES), bf16)
+
+        self.pass_on(0)
+
+    def ref(self, t, which=None, **way):
+        def make():
+            at = self.place.index(z=self.place.item(t)[0], **way)
+            return self.buf.at[at] if which is None else self.buf.at[at, self.half[which]]
+
+        return make
+
+    def ok(self, t):
+        return None if t == 0 else lambda: self.place.item(t)[1]
+
+    def same(self, ref, peer, slot, ok):
+        self.copies.start(ref, ref, peer, slot, ok)
+
+    def beside(self, **way):
+        return lambda: self.place.coords(**way)
+
+    def pass_on(self, t):
+        place = self.place
+        _, _, s, below = place.item(t)
+        for way in (1, -1) if t == 0 else ((1,) if below else (-1,)):
+            slot = 2 * s + 1 if way > 0 else 2 * s + 2
+
+            def inside(way=way):
+                there = place.z + way
+                good = (there >= 0) & (there < place.lines)
+                return good if t == 0 else good & place.item(t)[1]
+
+            if slot < self.items:
+                self.same(self.ref(t), lambda way=way: place.coords(z=place.z + way), self.Z + slot, inside)
+        ok = self.ok(t)
+        self.same(self.ref(t), self.beside(dx=1), self.X + t, ok)
+        self.same(self.ref(t), self.beside(dy=1), self.Y + t, ok)
+        self.same(self.ref(t), self.beside(dc=1), self.CZ + t, ok)
+
+    def at_distance(self, s):
+        return [0] if s == 0 else [2 * s - 1, 2 * s]
+
+    def along(self, s):
+        for t in self.at_distance(s):
+            self.copies.arrived(self.ref(t), self.Z + t, self.ok(t))
+            self.pass_on(t)
+
+    def across(self, s):
+        for t in self.at_distance(s):
+            ok = self.ok(t)
+            self.copies.arrived(self.ref(t, dx=1), self.X + t, ok)
+            self.same(self.ref(t, "a", dx=1), self.beside(dy=1), self.A + t, ok)
+            self.same(self.ref(t, dx=1), self.beside(dc=1), self.CX + t, ok)
+            self.copies.arrived(self.ref(t, dy=1), self.Y + t, ok)
+            self.same(self.ref(t, "b", dy=1), self.beside(dx=1), self.B + t, ok)
+            self.same(self.ref(t, dy=1), self.beside(dc=1), self.CY + t, ok)
+
+    def diagonal(self):
+        for t in range(self.items):
+            ok = self.ok(t)
+            self.copies.arrived(self.ref(t, "a", dy=1, dx=1), self.A + t, ok)
+            self.copies.arrived(self.ref(t, "b", dy=1, dx=1), self.B + t, ok)
+            self.same(self.ref(t, dy=1, dx=1), self.beside(dc=1), self.CD + t, ok)
+
+    def rest(self):
+        for t in range(self.items):
+            for k, way in ((self.CZ, {}), (self.CX, {"dx": 1}), (self.CY, {"dy": 1}), (self.CD, {"dy": 1, "dx": 1})):
+                self.copies.arrived(self.ref(t, dc=1, **way), k + t, self.ok(t))
+        self.copies.finish()
+
+
+class Scatter:
+    @staticmethod
+    def scratch(sect, inner):
+        lines = inner // 2
+        cut = half_of(sect.chunk)
+        return [
+            VM((4 * lines, sect.chunk, LANES), bf16),
+            VM((4 * lines, sect.chunk, LANES), bf16),
+            VM((2 * lines, cut, LANES), bf16),
+            VM((2 * lines, sect.chunk - cut, LANES), bf16),
+            VM((lines, sect.chunk - cut, LANES), bf16),
+            VM((lines, cut, LANES), bf16),
+            VM((lines, sect.chunk, LANES), bf16),
+            VM((sect.chunk, LANES), f32),
+            VM((sect.chunk, LANES), bf16),
+            VM((sect.slots, sect.chunk, LANES), bf16),
+            VM((sect.rows + 2 * sect.chunk + 16, LANES), f32),
+            pltpu.SemaphoreType.DMA((11 * lines + sect.sources,)),
+            pltpu.SemaphoreType.DMA((11 * lines + sect.slots,)),
+        ]
+
+    def __init__(self, sect, place, part_ref, scratch):
+        self.sect, self.place, self.partial = sect, place, part_ref
+        (self.work, self.rc, self.ry, self.rx, self.ry2, self.rx2, self.rz, self.frame, self.low, self.land, self.out,
+         send, recv) = scratch
+        self.copies = Copies(send, recv)
+        lines = place.lines
+        self.lines = lines
+        cut = half_of(sect.chunk)
+        self.a, self.b = pl.ds(0, cut), pl.ds(cut, sect.chunk - cut)
+        self.C, self.YA, self.XB, self.XA, self.YB, self.Z, self.O = (lines * k for k in (0, 4, 6, 8, 9, 10, 11))
+        self.order = [(dy, dx, d) for dy, dx in ((1, 1), (1, 0), (0, 1), (0, 0)) for d in self.far_first()]
+        self.steps = [self.core, self.first, self.second, self.third, self.settle, self.take]
+
+    def greet(self):
+        self.place.greet_all()
+
+    def far_first(self):
+        return list(range(1, self.lines)) + [0]
+
+    def z(self, d):
+        return lax.rem(self.place.z + d, self.lines) if d else self.place.z
+
+    def at(self, dy, dx, d):
+        return (dy * 2 + dx) * self.lines + d
+
+    def core(self):
+        place = self.place
+
+        def give(dy, dx, d):
+            k = self.at(dy, dx, d)
+            self.copies.start(
+                lambda: self.partial.at[place.index(dy=dy, dx=dx, z=self.z(d), dc=1)],
+                lambda: self.rc.at[k],
+                lambda: place.coords(dc=1),
+                self.C + k,
+            )
+
+        for spot in self.order:
+            give(*spot)
+
+    def send(self, k, rows, buf, n, way, slot):
+        self.copies.start(lambda: self.work.at[k, rows], lambda: buf.at[n], lambda: self.place.coords(**way), slot)
+
+    def got(self, buf, n, slot):
+        self.copies.arrived(lambda: buf.at[n], slot)
+
+    def plus(self, k, rows, other):
+        self.work[k, rows] = (self.work[k, rows].astype(f32) + other.astype(f32)).astype(bf16)
+
+    def first(self):
+        place, lines = self.place, self.lines
+        for dy, dx, d in self.order:
+            k = self.at(dy, dx, d)
+            self.got(self.rc, k, self.C + k)
+            mine = self.partial[place.index(dy=dy, dx=dx, z=self.z(d))]
+            self.work[k] = (mine.astype(f32) + self.rc[k].astype(f32)).astype(bf16)
+            if dy:
+                self.send(k, self.a, self.ry, dx * lines + d, {"dy": 1}, self.YA + dx * lines + d)
+            if dx:
+                self.send(k, self.b, self.rx, dy * lines + d, {"dx": 1}, self.XB + dy * lines + d)
+
+    def second(self):
+        lines = self.lines
+        for d in self.far_first():
+            n = lines + d
+            self.got(self.ry, n, self.YA + n)
+            self.plus(self.at(0, 1, d), self.a, self.ry[n])
+            self.send(self.at(0, 1, d), self.a, self.rx2, d, {"dx": 1}, self.XA + d)
+            self.got(self.rx, n, self.XB + n)
+            self.plus(self.at(1, 0, d), self.b, self.rx[n])
+            self.send(self.at(1, 0, d), self.b, self.ry2, d, {"dy": 1}, self.YB + d)
+
+    def third(self):
+        place = self.place
+        for d in self.far_first():
+            k = self.at(0, 0, d)
+            self.got(self.ry, d, self.YA + d)
+            self.got(self.rx, d, self.XB + d)
+            self.got(self.rx2, d, self.XA + d)
+            self.got(self.ry2, d, self.YB + d)
+            top = self.work[k, self.a].astype(f32) + self.ry[d].astype(f32) + self.rx2[d].astype(f32)
+            low = self.work[k, self.b].astype(f32) + self.rx[d].astype(f32) + self.ry2[d].astype(f32)
+            self.work[k, self.a] = top.astype(bf16)
+            self.work[k, self.b] = low.astype(bf16)
+            if d:
+                self.copies.start(
+                    lambda k=k: self.work.at[k],
+                    lambda d=d: self.rz.at[d],
+                    lambda d=d: place.coords(z=self.z(d)),
+                    self.Z + d,
+                )
+
+    def settle(self):
+        sect, me = self.sect, self.place.me
+        total = self.work[self.at(0, 0, 0)].astype(f32)
+        for d in range(1, self.lines):
+            self.got(self.rz, d, self.Z + d)
+            total = total + self.rz[d].astype(f32)
+        self.frame[...] = total
+        self.low[...] = total.astype(bf16)
+
+        def spread(per):
+            if per == 1:
+                return
+            tall = sect.chunk // per
+            for c in range(per):
+                self.out[pl.ds(c, tall, stride=per), :] = self.frame[c * tall : (c + 1) * tall, :]
+            self.low[...] = self.out[0 : sect.chunk, :].astype(bf16)
+
+        sect.by_kind(me, spread)
+        for s in range(sect.sources):
+            self.give(s)
+
+    def give(self, s):
+        sect, me = self.sect, self.place.me
+        i, ok = sect.of_chunk(me, s)
+
+        @pl.when(ok & (i == me))
+        def _():
+            self.land[sect.slot_of(me, i)] = self.low[...]
+
+        def owner():
+            return jnp.minimum(sect.of_chunk(me, s)[0], sect.count - 1)
+
+        def slot():
+            return jnp.clip(sect.slot_of(me, owner()), 0, sect.slots - 1)
+
+        def away():
+            i, ok = sect.of_chunk(me, s)
+            return ok & (i != me)
+
+        self.copies.start(
+            lambda: self.low, lambda: self.land.at[slot()], lambda: self.place.device(owner()), lambda: self.O + slot(), away
+        )
+
+    def take(self):
+        sect, me = self.sect, self.place.me
+        self.out[...] = jnp.zeros_like(self.out)
+        for k in range(sect.slots):
+            v, ok = sect.of_owner(me, k)
+            self.copies.arrived(lambda: self.land.at[k], self.O + k, lambda: ok & (v != me))
+
+            @pl.when(ok)
+            def _():
+                at = sect.chunk + sect.start(v) - sect.rows * me
+                self.out[pl.ds(at, sect.chunk), :] = self.land[k].astype(f32)
+
+        self.copies.finish()
+
+
+def all_steps(job):
+    for step in job.steps:
+        step()
+
+
+def pumped(steps, rows, points):
+    total, row = rows * points, pl.program_id(0)
+    due = {}
+    for k, step in enumerate(steps):
+        due.setdefault(k * (total - 1) // (len(steps) - 1), []).append(step)
+
+    def pump(point):
+        for r in range(rows):
+            for step in due.get(r * points + point, []):
+                pl.when(row == r)(step)
+
+    return pump
 
 
 def doc_marks(r, length, len_ref, dcol, tm, mb):
@@ -314,10 +729,11 @@
         ref[c, 8 + length : 16 + length, :] = jnp.zeros((8, LANES), f32)
 
 
-def fwd_kernel(length, len_ref, tok_ref, wp_ref, pw_ref, kw_ref, vec_ref,
+def fwd_kernel(length, pump, len_ref, tok_ref, wp_ref, pw_ref, kw_ref, vec_ref,
                qkvc_ref, kc_ref, dep_ref, ca_ref, tap_ref, join_ref, lse_ref,
                xs, cs, dcol, tm, mb, emat, acc):
     row = pl.program_id(0)
+    pump(0)
 
     @pl.when(row == 0)
     def _():
@@ -351,6 +767,7 @@
                     total = total + w[j] * (xs[c, at : at + step, :] * tm[j, r : r + step, :])
             dep_ref[r : r + step, c * LANES : (c + 1) * LANES] = total.astype(bf16)
 
+    pump(1)
     keyconv = nn(dep_ref[...], pw_ref[...]) + vec_ref[PB : PB + 1, 0:ATT]
     kc_ref[...] = keyconv.astype(bf16)
     ca = (keyconv * qkvc_ref[:, 0:ATT].astype(f32)).astype(bf16)
@@ -373,6 +790,7 @@
                 join_ref[:, ATT + c * LANES : ATT + (c + 1) * LANES] = part.astype(bf16)
 
     for p in range(3):
+        pump(2 + p)
         cols = slice(p * LANES, (p + 1) * LANES)
         q, k, v = (qkvc_ref[:, m * ATT + p * LANES : m * ATT + (p + 1) * LANES] for m in range(3))
         qs = q.astype(f32) * SCALE
@@ -389,6 +807,7 @@
             lse_ref[0, 2 * p + h : 2 * p + h + 1, :] = top + jnp.log(s)
             halves.append(o[h * HEAD_DIM : (h + 1) * HEAD_DIM, :] / s)
         join_ref[:, cols] = jnp.concatenate(halves, axis=0).T.astype(bf16)
+    pump(5)
 
 
 def blocked(rows, cols):
@@ -406,12 +825,29 @@
     ]
 
 
-def run_fwd(tokens, lengths, wp, pw, kw, vec):
+FWD_POINTS = 6
+
+
+def run_fwd(sect, outer, inner, own, tokens, lengths, wp, pw, kw, vec):
     rows, count = lengths.shape[0], tokens.shape[0]
     length = count // rows
-
-    def body(*refs):
-        fwd_kernel(length, *refs)
+    scratch = row_scratch(length) + [VM((length, ATT), f32)]
+    n = len(scratch)
+
+    def body(own_ref, *refs):
+        ours, (dw_ref, fi_ref, fo_ref) = refs[:13], refs[13:16]
+        job = Gather(sect, Place(outer, inner), own_ref, refs[16 + n :])
+
+        def begin():
+            job.greet()
+            job.steps[0]()
+
+        def end():
+            job.steps[-1]()
+            from_frames(job.buf, ((dw_ref, D, D, 0), (fi_ref, D, FF // GROUPS, 0), (fo_ref, FF, D // GROUPS, 0)))
+
+        pump = pumped([begin, *job.steps[1:-1], end], rows, FWD_POINTS)
+        fwd_kernel(length, pump, *ours, *refs[16 : 16 + n])
 
     full = pl.BlockSpec(memory_space=VM)
     return pl.pallas_call(
@@ -425,8 +861,11 @@
             jax.ShapeDtypeStruct((count, LANES), f32),
             jax.ShapeDtypeStruct((count, D), bf16),
             jax.ShapeDtypeStruct((rows, 8, length), f32),
+            jax.ShapeDtypeStruct((D, D), bf16),
+            jax.ShapeDtypeStruct((D, FF // GROUPS), bf16),
+            jax.ShapeDtypeStruct((FF, D // GROUPS), bf16),
         ],
-        in_specs=[pl.BlockSpec(memory_space=pltpu.SMEM), blocked(length, D), full, full, full, full],
+        in_specs=[full, pl.BlockSpec(memory_space=pltpu.SMEM), blocked(length, D), full, full, full, full],
         out_specs=[
             blocked(length, 4 * ATT),
             blocked(length, ATT),
@@ -435,16 +874,19 @@
             blocked(length, LANES),
             blocked(length, D),
             pl.BlockSpec((1, 8, length), lambda r: (r, 0, 0)),
+            full,
+            full,
+            full,
         ],
-        scratch_shapes=row_scratch(length) + [VM((length, ATT), f32)],
-        compiler_params=pltpu.CompilerParams(vmem_limit_bytes=VMEM_LIMIT),
+        scratch_shapes=scratch + Gather.scratch(sect, inner),
+        compiler_params=pltpu.CompilerParams(vmem_limit_bytes=VMEM_LIMIT, collective_id=2, has_side_effects=True),
         name="row_forward",
-    )(lengths, tokens, wp, pw, kw, vec)
+    )(own, lengths, tokens, wp, pw, kw, vec)
 
 
 def mid_kernel(length, len_ref, tok_ref, join_ref, cot_ref, dw_ref, fi_ref, fo_ref, vec_ref,
-               out_ref, gf_ref, gj_ref, gdw_ref, gfi_ref, gfo_ref, gv_ref,
-               xh1, rs1, nl, act, slope, gsec, gsl):
+               out_ref, gf_ref, gj_ref, part_ref, gv_ref,
+               gdw_ref, gfi_ref, gfo_ref, xh1, rs1, nl, act, slope, gsec, gsl, wide):
     row = pl.program_id(0)
     fg, dg = FF // GROUPS, D // GROUPS
 
@@ -460,7 +902,7 @@
     def vec(r, n=D):
         return vec_ref[r : r + 1, 0:n]
 
-    step = 64
+    step = 128
     gsec[...] = nn(join_ref[...], dw_ref[...])
 
     def norm1(i):
@@ -478,23 +920,23 @@
     tile = 512
     per = fg // tile
 
-    for g in range(GROUPS):
-        def widen(i, g=g):
-            col = pl.ds(pl.multiple_of(i * tile, tile), tile)
-            col2 = pl.ds(pl.multiple_of(g * fg + i * tile, tile), tile)
-            x = nn(nl[:, g * dg : (g + 1) * dg], fi_ref[g * dg : (g + 1) * dg, col]) + vec_ref[FIB : FIB + 1, col2]
-            e = jnp.exp(x * x * -0.5)
-            t = pl.reciprocal(1.0 + 0.2316419 * jnp.abs(x), approx=True)
-            poly = t * 0.53070271450 - 0.72657601350
-            poly = poly * t + 0.71070687050
-            poly = poly * t - 0.14224836800
-            poly = poly * t + 0.12741479600
-            q = poly * t * e
-            phi = jnp.where(x >= 0, 1.0 - q, q)
-            act[:, col2] = (x * phi).astype(bf16)
-            slope[:, col2] = (phi + x * 0.3989422804014327 * e).astype(bf16)
-
-        loop(per, widen)
+    tiles = [(g, i) for g in range(GROUPS) for i in range(per)]
+
+    def inner(n):
+        g, i = tiles[n]
+        wide[n % 2] = nn(nl[:, g * dg : (g + 1) * dg], fi_ref[g * dg : (g + 1) * dg, i * tile : (i + 1) * tile])
+
+    inner(0)
+    for n, (g, i) in enumerate(tiles):
+        if n + 1 < len(tiles):
+            inner(n + 1)
+        col = slice(g * fg + i * tile, g * fg + (i + 1) * tile)
+        for r in range(0, length, 64):
+            x = wide[n % 2, r : r + 64, :] + vec_ref[FIB : FIB + 1, col]
+            phi = 0.5 * lax.erf(x * math.sqrt(0.5)) + 0.5
+            e = jnp.exp2(x * x * (-0.5 / math.log(2.0)))
+            act[r : r + 64, col] = (x * phi).astype(bf16)
+            slope[r : r + 64, col] = (phi + x * (1.0 / math.sqrt(2.0 * math.pi)) * e).astype(bf16)
 
     for g in range(GROUPS):
         gsec[:, g * dg : (g + 1) * dg] = nn(act[:, g * fg : (g + 1) * fg], fo_ref[g * fg : (g + 1) * fg, :])
@@ -563,8 +1005,12 @@
     gj_ref[...] = nt(low, dw_ref[...]).astype(bf16)
     gdw_ref[...] += tn(join_ref[...], low)
 
-
-def run_mid(tokens, lengths, joined, cotangent, dw, fi, fo, vec):
+    @pl.when(row == pl.num_programs(0) - 1)
+    def _():
+        to_frames(part_ref, ((gdw_ref, D, D, 0), (gfi_ref, D, FF // GROUPS, 0), (gfo_ref, FF, D // GROUPS, 0)))
+
+
+def run_mid(sect, tokens, lengths, joined, cotangent, dw, fi, fo, vec):
     rows, count = lengths.shape[0], tokens.shape[0]
     length = count // rows
 
@@ -579,14 +1025,15 @@
             jax.ShapeDtypeStruct((count, D), bf16),
             jax.ShapeDtypeStruct((count, D), bf16),
             jax.ShapeDtypeStruct((count, D), bf16),
-            jax.ShapeDtypeStruct((D, D), f32),
-            jax.ShapeDtypeStruct((D, FF // GROUPS), f32),
-            jax.ShapeDtypeStruct((FF, D // GROUPS), f32),
+            jax.ShapeDtypeStruct((sect.count, sect.chunk, LANES), bf16),
             jax.ShapeDtypeStruct((VROWS, FF), f32),
         ],
         in_specs=[pl.BlockSpec(memory_space=pltpu.SMEM)] + [blocked(length, D)] * 3 + [full] * 4,
-        out_specs=[blocked(length, D)] * 3 + [full] * 4,
+        out_specs=[blocked(length, D)] * 3 + [full] * 2,
         scratch_shapes=[
+            VM((D, D), f32),
+            VM((D, FF // GROUPS), f32),
+            VM((FF, D // GROUPS), f32),
             VM((length, D), f32),
             VM((length, LANES), f32),
             VM((length, D), bf16),
@@ -594,17 +1041,19 @@
             VM((length, FF), bf16),
             VM((length, D), f32),
             VM((length, D), bf16),
+            VM((2, length, 512), f32),
         ],
         compiler_params=pltpu.CompilerParams(vmem_limit_bytes=VMEM_LIMIT),
         name="mid",
     )(lengths, tokens, joined, cotangent, dw, fi, fo, vec)
 
 
-def bwd_kernel(length, len_ref, tok_ref, qkvc_ref, kc_ref, dep_ref, ca_ref, tap_ref, join_ref, lse_ref, gf_ref, gj_ref,
+def bwd_kernel(length, pump, len_ref, tok_ref, qkvc_ref, kc_ref, dep_ref, ca_ref, tap_ref, join_ref, lse_ref, gf_ref, gj_ref,
                wp_ref, pw_ref, kw_ref, vec_ref,
                gt_ref, gp_ref, gpw_ref, gkw_ref, gv_ref,
                ds, cs, dcol, tm, mb, emat, gs, tp, prod, gq, gfour, acc):
     row = pl.program_id(0)
+    pump(0)
 
     @pl.when(row == 0)
     def _():
@@ -620,6 +1069,8 @@
         gv_ref[r : r + 1, 0 : value.shape[1]] += jnp.sum(value, axis=0, keepdims=True)
 
     for p in range(3):
+        if p:
+            pump(p)
         cols = slice(p * LANES, (p + 1) * LANES)
         q, k, v = (qkvc_ref[:, m * ATT + p * LANES : m * ATT + (p + 1) * LANES] for m in range(3))
         g = gj_ref[:, cols]
@@ -646,6 +1097,7 @@
         gfour[:, 2 * ATT + p * LANES : 2 * ATT + (p + 1) * LANES] = gv.astype(bf16)
         gv_ref[VB : VB + 1, cols] += jnp.sum(gv, axis=0, keepdims=True)
 
+    pump(3)
     for c in range(3):
         cs[c, 8 : 8 + length, :] = qkvc_ref[:, 3 * ATT + c * LANES : 3 * ATT + (c + 1) * LANES].astype(f32)
         gs[c, 8 : 8 + length, :] = gj_ref[:, ATT + c * LANES : ATT + (c + 1) * LANES].astype(f32)
@@ -684,6 +1136,7 @@
                 gfour[:, 3 * ATT + c * LANES : 3 * ATT + (c + 1) * LANES] = part.astype(bf16)
                 gv_ref[CB : CB + 1, c * LANES : (c + 1) * LANES] += jnp.sum(part, axis=0, keepdims=True)
 
+    pump(4)
     gkc = gca * qkvc_ref[:, 0:ATT].astype(f32)
     gquery = gq[...] + gca * kc_ref[...].astype(f32)
     add(QB, gquery)
@@ -698,6 +1151,7 @@
     for m in range(4):
         gp_ref[:, m * ATT : (m + 1) * ATT] += tn(tok_ref[...], gfour[:, m * ATT : (m + 1) * ATT])
 
+    pump(5)
     step = 64
     for c in range(6):
         cols = slice(c * LANES, (c + 1) * LANES)
@@ -722,15 +1176,40 @@
             gt_ref[r : r + step, cols] = total.astype(bf16)
         for j in range(KS):
             gv_ref[DW + KS - 1 - j : DW + KS - j, cols] += jnp.sum(sums[j], axis=0, keepdims=True)
-
-
-def run_bwd(tokens, lengths, saved, gf, gj, wp, pw, kw, vec):
+    pump(6)
+
+
+BWD_POINTS = 7
+
+
+def run_bwd(sect, outer, inner, part, tokens, lengths, saved, gf, gj, wp, pw, kw, vec):
     qkvc, kc, dep, ca, taps, joined, lse = saved
     rows, count = lengths.shape[0], tokens.shape[0]
     length = count // rows
-
-    def body(*refs):
-        bwd_kernel(length, *refs)
+    scratch = row_scratch(length) + [
+        VM((3, length + 16, LANES), f32),
+        VM((1, length + 16, LANES), f32),
+        VM((length, KS * ATT), bf16),
+        VM((length, ATT), f32),
+        VM((length, 4 * ATT), bf16),
+        VM((length, ATT), f32),
+    ]
+    n = len(scratch)
+
+    def body(part_ref, *refs):
+        ours, own_ref = refs[:20], refs[20]
+        job = Scatter(sect, Place(outer, inner), part_ref, refs[21 + n :])
+
+        def begin():
+            job.greet()
+            job.steps[0]()
+
+        def end():
+            job.steps[-1]()
+            own_ref[...] = job.out[sect.chunk : sect.chunk + sect.rows, :]
+
+        pump = pumped([begin, *job.steps[1:-1], end], rows, BWD_POINTS)
+        bwd_kernel(length, pump, *ours, *refs[21 : 21 + n])
 
     full = pl.BlockSpec(memory_space=VM)
     return pl.pallas_call(
@@ -742,8 +1221,10 @@
             jax.ShapeDtypeStruct((D, ATT), f32),
             jax.ShapeDtypeStruct((ATT, LANES), f32),
             jax.ShapeDtypeStruct((VROWS, FF), f32),
+            jax.ShapeDtypeStruct((sect.rows, LANES), f32),
         ],
         in_specs=[
+            full,
             pl.BlockSpec(memory_space=pltpu.SMEM),
             blocked(length, D),
             blocked(length, 4 * ATT),
@@ -760,43 +1241,92 @@
             full,
             full,
         ],
-        out_specs=[blocked(length, D)] + [full] * 4,
-        scratch_shapes=row_scratch(length)
-        + [
-            VM((3, length + 16, LANES), f32),
-            VM((1, length + 16, LANES), f32),
-            VM((length, KS * ATT), bf16),
-            VM((length, ATT), f32),
-            VM((length, 4 * ATT), bf16),
-            VM((length, ATT), f32),
+        out_specs=[blocked(length, D)] + [full] * 5,
+        scratch_shapes=scratch + Scatter.scratch(sect, inner),
+        compiler_params=pltpu.CompilerParams(vmem_limit_bytes=VMEM_LIMIT, collective_id=3, has_side_effects=True),
+        name="row_backward",
+    )(part, lengths, tokens, qkvc, kc, dep, ca, taps, joined, lse, gf, gj, wp, pw, kw, vec)
+
+
+def gather_kernel(sect, outer, inner, own_ref, wp_ref, pw_ref, kw_ref, vec_ref, flat, kwt, *scratch):
+    place = Place(outer, inner)
+    job = Gather(sect, place, own_ref, scratch)
+    job.greet()
+    all_steps(job)
+    pieces = [(wp_ref, D, ATT, m * ATT) for m in range(4)] + [(pw_ref, D, ATT, 0)]
+    v = from_frames(job.buf, pieces)
+    for n in range(sect.small):
+        flat[n * sect.chunk : (n + 1) * sect.chunk, :] = job.buf[v + n].astype(f32)
+    unpack_small(flat, kw_ref, vec_ref, kwt)
+
+
+def run_gather(sect, own, outer, inner):
+    def body(*refs):
+        gather_kernel(sect, outer, inner, *refs)
+
+    full = pl.BlockSpec(memory_space=VM)
+    return pl.pallas_call(
+        body,
+        out_shape=[
+            jax.ShapeDtypeStruct((D, 4 * ATT), bf16),
+            jax.ShapeDtypeStruct((D, ATT), bf16),
+            jax.ShapeDtypeStruct((ATT, LANES), bf16),
+            jax.ShapeDtypeStruct((VROWS, FF), f32),
         ],
-        compiler_params=pltpu.CompilerParams(vmem_limit_bytes=VMEM_LIMIT),
-        name="row_backward",
-    )(lengths, tokens, qkvc, kc, dep, ca, taps, joined, lse, gf, gj, wp, pw, kw, vec)
-
-
-def local_layer(tokens, lengths, cotangent, gathered, rows):
-    count = gathered.shape[0]
-    wp, pw, dw, fi, fo, kw, vec = run_unpack(gathered, rows)
-    saved = run_fwd(tokens, lengths, wp, pw, kw, vec)
-    output, gf, gj, gdw, gfi, gfo, va = run_mid(tokens, lengths, saved[5], cotangent, dw, fi, fo, vec)
-    gt, gp, gpw, gkw, vb = run_bwd(tokens, lengths, saved, gf, gj, wp, pw, kw, vec)
-    send = run_pack(count, rows, gp, gpw, gdw, gfi, gfo, gkw, va, vb)
-    return output, gt, send
+        in_specs=[full],
+        out_specs=[full] * 4,
+        scratch_shapes=[VM((sect.small * sect.chunk, LANES), f32), VM((512, LANES), f32)] + Gather.scratch(sect, inner),
+        compiler_params=pltpu.CompilerParams(vmem_limit_bytes=VMEM_LIMIT, collective_id=0, has_side_effects=True),
+        name="gather",
+    )(own)
+
+
+def scatter_kernel(sect, outer, inner, gp_ref, gpw_ref, gkw_ref, va_ref, vb_ref, other_ref, out_ref, part, vec, flat, kwt, *scratch):
+    place = Place(outer, inner)
+    job = Scatter(sect, place, part, scratch)
+    vec[...] = va_ref[...] + vb_ref[...]
+    v = to_frames(part, [(gp_ref, D, ATT, m * ATT) for m in range(4)] + [(gpw_ref, D, ATT, 0)])
+    pack_small(flat, gkw_ref, vec, kwt)
+    for n in range(sect.small):
+        part[v + n] = flat[n * sect.chunk : (n + 1) * sect.chunk, :].astype(bf16)
+    job.greet()
+    all_steps(job)
+    out_ref[...] = job.out[sect.chunk : sect.chunk + sect.rows, :] + other_ref[...]
+
+
+def run_scatter(sect, outer, inner, gp, gpw, gkw, va, vb, other):
+    def body(*refs):
+        scatter_kernel(sect, outer, inner, *refs)
+
+    full = pl.BlockSpec(memory_space=VM)
+    return pl.pallas_call(
+        body,
+        out_shape=jax.ShapeDtypeStruct((sect.rows, LANES), f32),
+        in_specs=[full] * 6,
+        out_specs=full,
+        scratch_shapes=[
+            VM((sect.count, sect.chunk, LANES), bf16),
+            VM((VROWS, FF), f32),
+            VM((max(sect.small * sect.chunk, 384), LANES), f32),
+            VM((512, LANES), f32),
+        ]
+        + Scatter.scratch(sect, inner),
+        compiler_params=pltpu.CompilerParams(vmem_limit_bytes=VMEM_LIMIT, collective_id=1, has_side_effects=True),
+        name="scatter",
+    )(gp, gpw, gkw, va, vb, other)
 
 
 def shards(tokens, doc_lengths, params, cotangent):
     rows = params.shape[0] // LANES
     outer, inner = lax.axis_size("dp"), lax.axis_size("fsdp")
-    count = outer * inner
-    pad = padded(rows)
-    own = jnp.pad(params.reshape(rows, LANES), ((0, pad - rows), (0, 0)))
-    gathered = lax.all_gather(own, ("dp", "fsdp"), axis=0, tiled=True).reshape(count, pad, LANES)
-    output, gt, send = local_layer(tokens, doc_lengths, cotangent, gathered, rows)
-    part = lax.psum_scatter(send.reshape(outer, inner, pad, LANES), "fsdp", scatter_dimension=1, tiled=True)
-    part = lax.psum_scatter(part, "dp", scatter_dimension=0, tiled=True).astype(f32)
-    part = lax.optimization_barrier(part.reshape(pad, LANES))
-    return output, gt, part[:rows].reshape(rows * LANES)
+    own = params.reshape(rows, LANES)
+    first, second = sections(outer * inner, rows, inner)
+    wp, pw, kw, vec = run_gather(first, own, outer, inner)
+    *saved, dw, fi, fo = run_fwd(second, outer, inner, own, tokens, doc_lengths, wp, pw, kw, vec)
+    output, gf, gj, part, va = run_mid(second, tokens, doc_lengths, saved[5], cotangent, dw, fi, fo, vec)
+    gt, gp, gpw, gkw, vb, some = run_bwd(second, outer, inner, part, tokens, doc_lengths, saved, gf, gj, wp, pw, kw, vec)
+    own_grad = run_scatter(first, outer, inner, gp, gpw, gkw, va, vb, some)
+    return output, gt, own_grad.reshape(rows * LANES)
 
 
 def solution(mesh):

time: 522 us -> 300 us (0.57)
  waiting for transfers between devices: 299 us -> 0 us
  Pallas kernels: 197 us -> 292 us
  between operations: 14 us -> 0.9 us
    unnamed x5 -> x0, waiting for transfers between devices: 214 us -> none
    all_gather x1 -> x0, waiting for transfers between devices: 84.3 us -> none  [shards(): lax.all_gather(own, ('dp', 'fsdp'), axis=0, tiled=True)]
    pallas_call x2, Pallas kernels: 21.3 us -> 90.5 us  [the longest x1 53.2 us: run_scatter(): pl.pallas_call(body, out_shape=jax.ShapeDtypeStruct((sect.rows, LANES), f...]
    pallas_call x1, Pallas kernels: 30.9 us -> 59.1 us  [run_fwd(): pl.pallas_call(body, grid=(rows,), out_shape=[jax.ShapeDtypeStruct((count...]
    pallas_call x1, Pallas kernels: 81.7 us -> 63.6 us  [run_mid(): pl.pallas_call(body, grid=(rows,), out_shape=[jax.ShapeDtypeStruct((count...]
    pallas_call x1, Pallas kernels: 62.6 us -> 78.8 us  [run_bwd(): pl.pallas_call(body, grid=(rows,), out_shape=[jax.ShapeDtypeStruct((count...]
  transfers between devices with their start and end apart: 3 -> 0, of which waited for: 3 -> 0; matrix products, arithmetic and copies ran while one was open for 0% -> 0% of each run, Pallas kernels for 0% -> 0%
where the time goes in v3:
time: 300 us; the launch traced here: 297 us
  Pallas kernels  292 us (97%)
  local copies, waits for them, and re-layouts  4.13 us (1%)
    pallas_call x1, Pallas kernels, run_bwd(): pl.pallas_call(body, grid=(rows,), out_shape=[jax.ShapeDtypeStruct((count...  78.8 us
    pallas_call x1, Pallas kernels, run_mid(): pl.pallas_call(body, grid=(rows,), out_shape=[jax.ShapeDtypeStruct((count...  63.6 us
    pallas_call x1, Pallas kernels, run_fwd(): pl.pallas_call(body, grid=(rows,), out_shape=[jax.ShapeDtypeStruct((count...  59.1 us
    pallas_call x1, Pallas kernels, run_scatter(): pl.pallas_call(body, out_shape=jax.ShapeDtypeStruct((sect.rows, LANES), f...  53.2 us
    pallas_call x1, Pallas kernels, run_gather(): pl.pallas_call(body, out_shape=[jax.ShapeDtypeStruct((D, 4 * ATT), bf16),...  37.4 us

profile of v3, /device:TPU:2, one launch (start us, length us, event | category | flops | bytes accessed | tf_op | source)
XLA Modules:
  0.0 296.9 jit_solution(269980223555446294)
XLA Ops:
  0.6 37.4 %gather.1 = (bf16[768,1536]{1,0:T(8,128)(2,1)}, bf16[768,384]{1,0:T(8,128)(2,1)}, bf16[384,128]{1,0:T(8,128)(2,1)}, f32[24,3072]{1,0:T(8,128)}) custom-call(bf16[1090,128]{1,0:T(8,128)(2,1)} %bitcast.3), custom_call_target="tpu_custom_call" | custom-call | tf_op jit(solution)/shard_map/gather/pallas_call | solution.py:1268
  38.0 59.1 %row_forward.1 = (bf16[1536,1536]{1,0:T(8,128)(2,1)}, bf16[1536,384]{1,0:T(8,128)(2,1)}, bf16[1536,768]{1,0:T(8,128)(2,1)}, bf16[1536,384]{1,0:T(8,128)(2,1)}, f...) custom-call(bf16[1090,128]{1,0:T(8,128)(2,1)} %bitcast.4, ...), custom_call_target="tpu_custom_call" | custom-call | tf_op jit(solution)/shard_map/row_forward/pallas_call | solution.py:853
  97.1 63.6 %mid.1 = (bf16[1536,768]{1,0:T(8,128)(2,1)}, bf16[1536,768]{1,0:T(8,128)(2,1)}, bf16[1536,768]{1,0:T(8,128)(2,1)}, bf16[32,768,128]{2,1,0:T(8,128)(2,1)}, f32[24,3072]{1,0:T(8,128)}) custom-call(s32[3,16]{1,0:T(4,128)} %refs_0_.5, bf16[1536,768]{1,0:T(8,128)(2,1)} %refs_1_.5, bf16[1536,768]{1,0:T(8,128)(2,1)} %get-tuple-element.32.refs_2_.refs_7_, ...), custom_call_target="tpu_custom_call" | custom-call | tf_op jit(solution)/shard_map/mid/pallas_call | solution.py:1021
  160.7 78.8 %row_backward.1 = (bf16[1536,768]{1,0:T(8,128)(2,1)}, f32[768,1536]{1,0:T(8,128)}, f32[768,384]{1,0:T(8,128)}, f32[384,128]{1,0:T(8,128)}, f32[24,3072]{1,0:T(8,128)}, /*index=5*/f32[1090,128]{1,0:T(8,128)}) custom-call(bf16[32,768,128]{2,1,0:T(8,128)(2,1)} %get-tuple-element.37.part_ref, s32[3,16]{1,0:T(4,128)} %refs_0_.5, bf16[1536,768]{1,0:T(8,128)(2,1)} %refs_1_.5, ...), custom_call_target="tpu_custom_call" | custom-call | tf_op jit(solution)/shard_map/row_backward/pallas_call | solution.py:1215
  239.4 53.2 %scatter.1 = f32[1090,128]{1,0:T(8,128)} custom-call(f32[768,1536]{1,0:T(8,128)} %get-tuple-element.47.refs_0_, f32[768,384]{1,0:T(8,128)} %get-tuple-element.48.refs_1_, f32[384,128]{1,0:T(8,128)} %get-tuple-element.49.refs_2_, f32[24,3072]{1,0:T(8,128)} %get-tuple-element.50.refs_3_, f32[24,3072]{1,0:T(8,128)} %get-tuple-element.51.refs_4_, ...), custom_call_target="tpu_custom_call" | custom-call | tf_op jit(solution)/shard_map/scatter/pallas_call | solution.py:1302
  292.6 0.0 copy-start
  292.6 3.3 %copy.9 = bf16[1536,768]{1,0:T(8,128)(2,1)} copy(bf16[1536,768]{1,0:T(8,128)(2,1)} %get-tuple-element.57) | data formatting | bytes 4718592
  295.9 0.0 copy-done
  295.9 0.8 copy.10
Async XLA Ops:
  292.6 3.3 %copy-start = (f32[1090,128]{1,0:T(8,128)S(1)}, f32[1090,128]{1,0:T(8,128)}, u32[]{:S(2)}) copy-start(f32[1090,128]{1,0:T(8,128)} %scatter.1) | copy-start | bytes 1674244
